TPU v7x, 32 devices: a whole 2x2x4 slice. The times are simulated.
32 devices in a mesh: pipe: 2 (over y), dp: 4 (over z), tensor: 4 (over x, core).
Axes of the slice: x: 2, y: 2, z: 4, core: 2. Of those that a mesh axis runs over, the one named last changes fastest.
Arguments:
- tokens: bfloat16 [3072, 8192], P(('pipe', 'dp'), 'tensor'), parts along dimension 0, may hold values from -6 to 6
- pattern: int32 [128, 6], P('pipe'), parts along dimension 0, may hold values from 0 to 31, as said below
- blocks: bfloat16 [128, 6, 256, 256], P(('pipe', 'tensor'), None, 'dp'), parts along dimension 0, may hold values from -0.15625 to 0.15625
- left_factor: bfloat16 [16384, 512], P(('pipe', 'tensor'), 'dp'), parts along dimension 0, may hold values from -0.0625 to 0.0625
- right_factor: bfloat16 [1024, 16384], P(('pipe', 'dp'), 'tensor'), parts along dimension 0, may hold values from -0.25 to 0.25
- cotangent: bfloat16 [3072, 16384], P(('pipe', 'dp'), 'tensor'), parts along dimension 0, may hold values from -6 to 6
Outputs:
- hidden: bfloat16 [3072, 16384], P(('pipe', 'dp'), 'tensor'), parts along dimension 0
- token_grad: float32 [3072, 8192], P(('pipe', 'dp'), 'tensor'), parts along dimension 0
- block_grad: float32 [128, 6, 256, 256], P(('pipe', 'tensor'), None, 'dp'), parts along dimension 0
- left_grad: float32 [16384, 512], P(('pipe', 'tensor'), 'dp'), parts along dimension 0
- right_grad: float32 [1024, 16384], P(('pipe', 'dp'), 'tensor'), parts along dimension 0
There are 2 independent parts, one for each index of `pipe`. A program takes and returns all parts, laid end to end along the dimension named above; each array names one. Nothing has to cross between parts.
Inputs may be any that keep to these rules, and one draw needn't show every extreme that they name: `pattern`: row j lists the 6 input blocks feeding hidden block j: under a relabeling of the 32 input blocks drawn from the seed, they are the labels of (j mod 32) XOR s for s = 0 and then the powers of two below 32 in rising order; a row's entries are distinct.
All inputs are finite; a program needn't handle non-finite values.
Results may differ from a plain program's by a relative error of at most 0.017.
Values may be sent and summed in bfloat16 or wider, within the bound.
A program may use at most 256 MiB of HBM per device.

v0:
```python
import jax
import jax.numpy as jnp
from jax import lax
from jax.sharding import PartitionSpec as P

SQRT_HALF = 0.7071067811865476
INV_ROOT_TWO_PI = 0.3989422804014327


def gelu_parts(preact):
    normal_cdf = 0.5 * (1.0 + jax.scipy.special.erf(preact * SQRT_HALF))
    return (
        preact * normal_cdf,
        normal_cdf + preact * jnp.exp(-0.5 * preact * preact) * INV_ROOT_TWO_PI,
    )


def per_device(tokens, pattern, blocks, left_factor, right_factor, cotangent):
    tok_rows = tokens.shape[0]
    block_size = blocks.shape[3]
    local_cols = blocks.shape[0]
    slot_count = blocks.shape[1]
    full_tokens = lax.all_gather(tokens, "tensor", axis=1, tiled=True)
    block_count = full_tokens.shape[1] // block_size
    tensor_rank = lax.axis_index("tensor")
    local_pattern = lax.dynamic_slice_in_dim(pattern, tensor_rank * local_cols, local_cols, 0)
    picked = jnp.take(full_tokens.reshape(tok_rows, block_count, block_size), local_pattern, axis=1)
    inputs = picked
    butterfly = jnp.einsum(
        "tjkc,jkcd->tjd",
        inputs,
        lax.all_gather(blocks, "dp", axis=2, tiled=True),
        preferred_element_type=jnp.float32,
    )
    left_rows = lax.all_gather(left_factor, "dp", axis=1, tiled=True)
    whole_left = lax.all_gather(left_rows, "tensor", axis=0, tiled=True)
    rank_acts = jnp.dot(full_tokens, whole_left, preferred_element_type=jnp.float32).astype(
        jnp.bfloat16
    )
    inputs = rank_acts
    rank_part = jnp.dot(
        inputs,
        lax.all_gather(right_factor, "dp", axis=0, tiled=True),
        preferred_element_type=jnp.float32,
    )
    preact = butterfly.reshape(tok_rows, -1) + rank_part
    activated, slope_values = gelu_parts(preact)
    hidden = activated.astype(jnp.bfloat16)
    grad_pre = (cotangent.astype(jnp.float32) * slope_values).astype(jnp.bfloat16)
    rank_terms = lax.dot_general(
        grad_pre,
        lax.all_gather(right_factor, "dp", axis=0, tiled=True),
        (((1,), (1,)), ((), ())),
        preferred_element_type=jnp.float32,
    )
    rank_grad = lax.psum(rank_terms.astype(jnp.bfloat16), "tensor")
    right_term = lax.dot_general(
        rank_acts, grad_pre, (((0,), (0,)), ((), ())), preferred_element_type=jnp.float32
    )
    right_grad = lax.psum_scatter(
        right_term.astype(jnp.bfloat16), "dp", scatter_dimension=0, tiled=True
    ).astype(jnp.float32)
    left_term = lax.dot_general(
        tokens, rank_grad, (((0,), (0,)), ((), ())), preferred_element_type=jnp.float32
    )
    left_grad = lax.psum_scatter(
        left_term.astype(jnp.bfloat16), "dp", scatter_dimension=1, tiled=True
    ).astype(jnp.float32)
    grad_blocks = grad_pre.reshape(tok_rows, local_cols, block_size)
    block_term = jnp.einsum(
        "tjkc,tjd->jkcd", picked, grad_blocks, preferred_element_type=jnp.float32
    )
    block_grad = lax.psum_scatter(
        block_term.astype(jnp.bfloat16), "dp", scatter_dimension=2, tiled=True
    ).astype(jnp.float32)
    spread = jnp.einsum(
        "tjd,jkcd->tjkc",
        grad_blocks,
        lax.all_gather(blocks, "dp", axis=2, tiled=True),
        preferred_element_type=jnp.float32,
    )
    placed = (
        jnp.zeros((tok_rows, block_count, block_size), jnp.float32)
        .at[:, local_pattern.reshape(-1)]
        .add(spread.reshape(tok_rows, local_cols * slot_count, block_size))
    )
    token_part = lax.psum_scatter(
        placed.reshape(tok_rows, -1).astype(jnp.bfloat16), "tensor", scatter_dimension=1, tiled=True
    ).astype(jnp.float32)
    token_grad = token_part + lax.dot_general(
        rank_grad, left_rows, (((1,), (1,)), ((), ())), preferred_element_type=jnp.float32
    )
    return (hidden, token_grad, block_grad, left_grad, right_grad)


def solution(mesh):
    placed = (
        P(("pipe", "dp"), "tensor"),
        P("pipe", None),
        P(("pipe", "tensor"), None, "dp", None),
        P(("pipe", "tensor"), "dp"),
        P(("pipe", "dp"), "tensor"),
        P(("pipe", "dp"), "tensor"),
    )
    return jax.shard_map(
        per_device,
        mesh=mesh,
        in_specs=placed,
        out_specs=(
            P(("pipe", "dp"), "tensor"),
            P(("pipe", "dp"), "tensor"),
            P(("pipe", "tensor"), None, "dp", None),
            P(("pipe", "tensor"), "dp"),
            P(("pipe", "dp"), "tensor"),
        ),
        check_vma=False,
    )
```

profile of v0, /device:TPU:0, one launch (start us, length us, event | category | flops | bytes accessed | tf_op | source)
XLA Modules:
  0.0 936.9 jit_solution(5141369474184893608)
XLA Ops:
  7.2 0.7 all-gather.10.cloned.1.call-update
  7.9 0.0 all-gather.6.cloned.1.call-start
  8.0 2.6 copy.32
  10.6 0.0 all-gather.12.cloned.1.call-start
  10.6 47.9 %all-gather.10.cloned.1.call-done = bf16[2048,512]{1,0:T(8,128)(2,1)} async-done(((bf16[2048,128]{1,0:T(8,128)(2,1)}), bf16[2048,512]{1,0:T(8,128)(2,1)}) %all-gather.10.cloned.1.call-update) | async-done | bytes 2097168 | tf_op jit(solution)/shard_map/all_gather | solution.py:35
  58.6 0.0 all-gather.8.cloned.1.call-start
  58.6 0.5 all-gather.8.cloned.1.call-update
  59.2 0.5 all-gather.14.cloned.1.call-update
  59.7 0.0 all-reduce.2.cloned.1.call-start
  59.8 0.1 compare_and_fusion
  59.9 0.1 copy.31
  60.0 0.1 copy.33
  60.1 0.1 reshape.67
  60.2 45.2 %all-gather.6.cloned.1.call-done = bf16[384,8192]{0,1:T(8,128)(2,1)} async-done(((bf16[384,2048]{0,1:T(8,128)(2,1)}), bf16[384,8192]{0,1:T(8,128)(2,1)}) %all-gather.6.cloned.1.call-update) | async-done | bytes 6291472 | tf_op jit(solution)/shard_map/all_gather | solution.py:23
  105.3 8.6 copy.34
  114.0 13.0 %gather_fusion = bf16[96,384,256]{2,1,0:T(8,128)(2,1)} fusion(bf16[384,32,256]{2,0,1:T(8,128)(2,1)} %copy.34, s32[1024]{0:T(1024)S(1)} %pad_clamp_fusion), kind=kCustom, calls=%fused_computation | custom fusion | bytes 37749120 | tf_op jit(solution)/shard_map/jit(_take)/gather | solution.py:27
  126.9 24.7 %copy.35 = bf16[16,6,384,256]{2,3,1,0:T(8,128)(2,1)} copy(bf16[16,6,384,256]{3,2,1,0:T(8,128)(2,1)} %bitcast.47) | data formatting | bytes 37748736 | tf_op jit(solution)/shard_map/jit(_take)/gather | solution.py:27
  151.6 13.6 %all-gather.12.cloned.1.call-done = bf16[8192,512]{1,0:T(8,128)(2,1)} async-done(((bf16[2048,512]{1,0:T(8,128)(2,1)}), bf16[8192,512]{1,0:T(8,128)(2,1)}) %all-gather.12.cloned.1.call-update) | async-done | bytes 8388624 | tf_op jit(solution)/shard_map/all_gather | solution.py:36
  165.2 8.6 convolution_convert_fusion.3
  173.8 211.0 %all-gather.8.cloned.1.call-done = bf16[16,6,256,256]{3,2,1,0:T(8,128)(2,1)} async-done(((bf16[16,6,64,256]{3,2,1,0:T(8,128)(2,1)}), bf16[16,6,256,256]{3,2,1,0:T(8,128)(2,1)}) %all-gather.8.cloned.1.call-update) | async-done | bytes 12582928 | tf_op jit(solution)/shard_map/all_gather | solution.py:32
  384.9 16.6 %fusion.2 = f32[16,384,256,1]{1,2,3,0:T(8,128)} fusion(bf16[16,6,256,256]{3,2,1,0:T(8,128)(2,1)} %all-gather.8.cloned.1.call-done, bf16[16,6,384,256]{2,3,1,0:T(8,128)(2,1)} %copy.35, pred[16,6]{1,0:T(8,128)(4,1)S(1)} %copy.31), kind=kOutput, calls=%fused_computation.4 | convolution fusion | flops 4841275392 | bytes 37748832 | tf_op jit(solution)/shard_map/tjkc,jkcd->tjd/dot_general | solution.py:29
  401.5 6.6 copy.37
  408.1 57.2 %all-gather.14.cloned.1.call-done = bf16[512,4096]{1,0:T(8,128)(2,1)} async-done(((bf16[128,4096]{1,0:T(8,128)(2,1)}), bf16[512,4096]{1,0:T(8,128)(2,1)}) %all-gather.14.cloned.1.call-update) | async-done | bytes 4194320 | tf_op jit(solution)/shard_map/all_gather | solution.py:43
  465.3 10.5 %fusion.14 = (bf16[384,4096]{1,0:T(8,128)(2,1)S(1)}, bf16[384,4096]{1,0:T(8,128)(2,1)}) fusion(bf16[384,4096]{1,0:T(8,128)(2,1)} %param.11, f32[384,4096]{1,0:T(8,128)} %copy.37, bf16[384,512]{1,0:T(8,128)(2,1)S(1)} %convolution_convert_fusion.3, bf16[512,4096]{1,0:T(8,128)(2,1)} %all-gather.14.cloned.1.call-done), kind=kOutput, calls=%fused_computation.16 | convolution fusion | flops 1632632832 | bytes 20316160 | tf_op jit(solution)/shard_map/dot_general | solution.py:41
  475.8 2.6 convolution_convert_fusion.2
  478.5 0.2 reduce-scatter.9.cloned.1.call-start
  478.7 31.1 %all-reduce.2.cloned.1.call-done = bf16[384,512]{1,0:T(8,128)(2,1)} async-done(((bf16[384,512]{1,0:T(8,128)(2,1)}), bf16[384,512]{1,0:T(8,128)(2,1)}) %all-reduce.2.cloned.1.call-update) | async-done | bytes 393232 | tf_op jit(solution)/shard_map/psum | solution.py:56
  509.8 4.1 fusion.18
  513.9 0.0 reduce-scatter.11.cloned.1.call-start
  514.0 4.4 convolution_convert_fusion
  518.5 0.0 reduce-scatter.5.cloned.1.call-start
  518.5 0.1 copy.38
  518.6 0.1 reshape.62
  518.7 3.3 copy.52
  522.0 25.2 %fusion.16 = f32[16,384,6,256]{3,1,2,0:T(8,128)} fusion(bf16[16,6,256,256]{3,2,1,0:T(8,128)(2,1)} %all-gather.8.cloned.1.call-done, bf16[384,16,256,1]{2,1,0,3:T(8,128)(2,1)S(1)} %bitcast.50), kind=kOutput, calls=%fused_computation.25 | convolution fusion | flops 4831838208 | bytes 53477376 | tf_op jit(solution)/shard_map/tjd,jkcd->tjkc/dot_general | solution.py:76
  547.2 5.9 broadcast_in_dim.19
  553.1 90.2 %scatter_fusion = f32[384,32,256]{2,0,1:T(8,128)} fusion(f32[384,32,256]{2,0,1:T(8,128)} %broadcast_in_dim.19, s32[96]{0:T(128)S(1)} %fusion.19, f32[96,384,256]{2,1,0:T(8,128)} %bitcast.46), kind=kCustom, calls=%fused_computation.1 | custom fusion | flops 9437184 | bytes 113246592 | tf_op jit(solution)/shard_map/scatter-add | solution.py:85
  643.3 5.4 convert_bitcast_fusion
  648.7 3.5 copy.51
  652.3 0.3 reduce-scatter.7.cloned.1.call-start
  652.5 1.6 copy-done.1
  654.1 15.2 %fusion.6 = bf16[16,6,256,256]{3,2,1,0:T(8,128)(2,1)} fusion(bf16[16,6,384,256]{2,3,1,0:T(8,128)(2,1)} %copy.35, pred[16,6]{1,0:T(8,128)(4,1)S(1)} %copy.31, bf16[384,16,256,1]{2,1,0,3:T(8,128)(2,1)S(1)} %bitcast.51), kind=kOutput, calls=%fused_computation.10 | convolution fusion | flops 4847566848 | bytes 34603104 | tf_op jit(solution)/shard_map/tjkc,tjd->jkcd/dot_general | solution.py:70
  669.4 2.4 copy.42
  671.8 2.8 convert_element_type.59
  674.6 35.9 %reduce-scatter.5.cloned.1.call-done = bf16[384,2048]{1,0:T(8,128)(2,1)} async-done(((bf16[384,8192]{1,0:T(8,128)(2,1)}), bf16[384,2048]{1,0:T(8,128)(2,1)}) %reduce-scatter.5.cloned.1.call-update) | async-done | bytes 1572880 | tf_op jit(solution)/shard_map/reduce_scatter | solution.py:87
  710.5 4.1 convert_add_fusion
  714.6 210.0 %reduce-scatter.7.cloned.1.call-done = bf16[16,6,64,256]{3,2,1,0:T(8,128)(2,1)} async-done(((bf16[16,6,256,256]{3,2,1,0:T(8,128)(2,1)}), bf16[16,6,64,256]{3,2,1,0:T(8,128)(2,1)}) %reduce-scatter.7.cloned.1.call-update) | async-done | bytes 3145744 | tf_op jit(solution)/shard_map/reduce_scatter | solution.py:73
  924.6 5.5 convert_element_type.54
  (27 shorter events, 0.3 us)
Async XLA Ops:
  7.2 52.6 %copy-start.5 = (s32[64,6]{0,1:T(8,128)S(1)}, s32[64,6]{0,1:T(8,128)}, u32[]{:S(2)}) copy-start(s32[64,6]{0,1:T(8,128)} %param.7) | copy-start | bytes 4612
  7.2 51.4 %all-gather.10.cloned.1.call-start = ((), (), s32[]{:S(2)}) async-start(), calls=%async_computation.6 | async-start | bytes 2621440 | tf_op jit(solution)/shard_map/all_gather | solution.py:35
  7.9 97.4 %all-gather.6.cloned.1.call-start = ((), (), s32[]{:S(2)}) async-start(), calls=%async_computation.4 | async-start | bytes 7864320 | tf_op jit(solution)/shard_map/all_gather | solution.py:23
  10.6 154.6 %all-gather.12.cloned.1.call-start = ((), (), s32[]{:S(2)}) async-start(), calls=%async_computation.7 | async-start | bytes 10485760 | tf_op jit(solution)/shard_map/all_gather | solution.py:36
  58.6 326.3 %all-gather.8.cloned.1.call-start = ((), (), s32[]{:S(2)}) async-start(), calls=%async_computation.5 | async-start | bytes 15728640 | tf_op jit(solution)/shard_map/all_gather | solution.py:32
  59.1 406.1 %all-gather.14.cloned.1.call-start = ((), (), s32[]{:S(2)}) async-start(), calls=%async_computation.8 | async-start | bytes 5242880 | tf_op jit(solution)/shard_map/all_gather | solution.py:43
  59.7 450.0 %all-reduce.2.cloned.1.call-start = ((), (), s32[]{:S(2)}) async-start(), calls=%async_computation.10 | async-start | bytes 786432 | tf_op jit(solution)/shard_map/psum | solution.py:56
  465.3 10.5 %copy-start.6 = (bf16[512,4096]{1,0:T(8,128)(2,1)S(1)}, bf16[512,4096]{1,0:T(8,128)(2,1)}, u32[]{:S(2)}) copy-start(bf16[512,4096]{1,0:T(8,128)(2,1)} %all-gather.14.cloned.1.call-done) | copy-start | bytes 12582916
  475.8 38.2 %copy-start.2 = (bf16[384,4096]{1,0:T(8,128)(2,1)}, bf16[384,4096]{1,0:T(8,128)(2,1)S(1)}, u32[]{:S(2)}) copy-start(bf16[384,4096]{1,0:T(8,128)(2,1)S(1)} %get-tuple-element.22) | copy-start | bytes 9437188
  478.5 190.9 %reduce-scatter.9.cloned.1.call-start = ((), (), s32[]{:S(2)}) async-start(), calls=%async_computation.12 | async-start | bytes 2621440 | tf_op jit(solution)/shard_map/reduce_scatter | solution.py:66
  513.9 157.8 %reduce-scatter.11.cloned.1.call-start = ((), (), s32[]{:S(2)}) async-start(), calls=%async_computation.13 | async-start | bytes 5242880 | tf_op jit(solution)/shard_map/reduce_scatter | solution.py:60
  518.5 192.0 %reduce-scatter.5.cloned.1.call-start = ((), (), s32[]{:S(2)}) async-start(), calls=%async_computation.9 | async-start | bytes 7864320 | tf_op jit(solution)/shard_map/reduce_scatter | solution.py:87
  522.0 25.2 %copy-start = (bf16[48,8,16,256]{3,2,1,0:T(8,128)(2,1)}, bf16[48,8,16,256]{3,2,1,0:T(8,128)(2,1)S(1)}, u32[]{:S(2)}) copy-start(bf16[48,8,16,256]{3,2,1,0:T(8,128)(2,1)S(1)} %copy.52) | copy-start | bytes 9437188
  652.3 1.9 copy-start.1
  652.3 272.3 %reduce-scatter.7.cloned.1.call-start = ((), (), s32[]{:S(2)}) async-start(), calls=%async_computation.11 | async-start | bytes 15728640 | tf_op jit(solution)/shard_map/reduce_scatter | solution.py:73
  669.3 41.1 %copy-start.3 = (bf16[2048,512]{1,0:T(8,128)(2,1)S(1)}, bf16[2048,512]{1,0:T(8,128)(2,1)}, u32[]{:S(2)}) copy-start(bf16[2048,512]{1,0:T(8,128)(2,1)} %all-gather.10.cloned.1.call-done) | copy-start | bytes 6291460
  669.3 41.1 %copy-start.4 = (bf16[384,512]{1,0:T(8,128)(2,1)S(1)}, bf16[384,512]{1,0:T(8,128)(2,1)}, u32[]{:S(2)}) copy-start(bf16[384,512]{1,0:T(8,128)(2,1)} %all-reduce.2.cloned.1.call-done) | copy-start | bytes 1179652
Sparse Core Ops, SparseCore 0:
  9.6 48.9 all-gather.9
  60.7 44.5 all-gather.5
  106.9 58.2 all-gather.11
  166.6 218.2 all-gather.7
  386.3 78.9 all-gather.13
  478.6 31.1 all-reduce.1
  514.0 43.8 reduce-scatter.8
  560.2 76.0 reduce-scatter.10
  652.4 58.0 reduce-scatter.4
  712.7 211.8 reduce-scatter.6
where the time goes:
time: 939 us; the launch traced here: 937 us
  waiting for transfers between devices  654 us (70%)
  other arithmetic  104 us (11%)
  matrix products  91.4 us (10%)
  local copies, waits for them, and re-layouts  72.6 us (8%)
  between operations  14.3 us (2%)
    all_gather x1, waiting for transfers between devices, per_device(): lax.all_gather(blocks, 'dp', axis=2, tiled=True)  211 us
    reduce_scatter x1, waiting for transfers between devices, per_device(): lax.psum_scatter(block_term.astype(jnp.bfloat16), 'dp', scatter_dimension...  210 us
    scatter-add x1, other arithmetic, per_device(): placed = jnp.zeros((tok_rows, block_count, block_size), jnp.float32).at[:...  90.2 us
    all_gather x1, waiting for transfers between devices, per_device(): lax.all_gather(right_factor, 'dp', axis=0, tiled=True)  57.2 us
    all_gather x1, waiting for transfers between devices, per_device(): left_rows = lax.all_gather(left_factor, 'dp', axis=1, tiled=True)  47.9 us
    all_gather x1, waiting for transfers between devices, per_device(): full_tokens = lax.all_gather(tokens, 'tensor', axis=1, tiled=True)  45.2 us
    gather x2, local copies, waits for them, and re-layouts, per_device(): jnp.take(full_tokens.reshape(tok_rows, block_count, block_size), local_pa...  37.6 us
    reduce_scatter x1, waiting for transfers between devices, per_device(): lax.psum_scatter(placed.reshape(tok_rows, -1).astype(jnp.bfloat16), 'tens...  35.9 us
  transfers between devices with their start and end apart: 10, of which 8 were waited for; matrix products, arithmetic and copies ran while one was open for 26% of the time, Pallas kernels for 0%

commit v1 on v0

v1 whole, which is shorter than its diff:
```python
import functools

import jax
import jax.numpy as jnp
from jax import lax
from jax.experimental import pallas as pl
from jax.experimental.pallas import tpu as pltpu
from jax.sharding import PartitionSpec as P

SQRT_HALF = 0.7071067811865476
INV_ROOT_TWO_PI = 0.3989422804014327
CHUNKS = 4
F32 = jnp.float32
BF16 = jnp.bfloat16


def line_gather(own, n):
    from_left, from_right = {}, {}
    for m in range(1, n):
        right_pairs = [(d, d + 1) for d in range(n - 1) if d - (m - 1) >= 0]
        left_pairs = [(d, d - 1) for d in range(1, n) if d + (m - 1) <= n - 1]
        from_left[m] = lax.ppermute(own if m == 1 else from_left[m - 1], "dp", right_pairs)
        from_right[m] = lax.ppermute(own if m == 1 else from_right[m - 1], "dp", left_pairs)
    return [(from_left[m], from_right[n - m]) for m in range(1, n)]


def line_scatter(terms, n):
    got_left = got_right = None
    for m in range(n - 1, 0, -1):
        right_pairs = [(d, d + 1) for d in range(n - 1) if d + m <= n - 1]
        left_pairs = [(d, d - 1) for d in range(1, n) if d - m >= 0]
        to_right = terms[m] if got_left is None else terms[m] + got_left
        to_left = terms[n - m] if got_right is None else terms[n - m] + got_right
        got_left = lax.ppermute(to_right, "dp", right_pairs)
        got_right = lax.ppermute(to_left, "dp", left_pairs)
    return terms[0].astype(F32) + got_left.astype(F32) + got_right.astype(F32)


def chunk_kernel(n, slots, bs, first, base, where_ref, pattern_ref, x_ref, xt_ref, ra_ref, rat_ref, cot_ref, *rest):
    own_ref = rest[0]
    pairs = [(rest[1 + 2 * i], rest[2 + 2 * i]) for i in range(n - 1)]
    rest = rest[1 + 2 * (n - 1) :]
    if not first:
        acc_in, _ = rest[:2]
        rest = rest[2:]
    hid_ref, acc_ref = rest[:2]
    term_refs = rest[2 : 2 + n]
    w_ref, r_ref, bt_ref = rest[2 + n :]
    step = pl.program_id(0)
    me = where_ref[0]
    cs = bs // n
    rs = ra_ref.shape[1] // n
    width = x_ref.shape[1]

    @pl.when(step == 0)
    def _():
        if first:
            acc_ref[...] = jnp.zeros_like(acc_ref)
        else:
            pltpu.sync_copy(acc_in, acc_ref)

    for m in range(n):
        row = pl.multiple_of(lax.rem(me + n - m, n) * cs, cs)
        for k in range(slots + 1):
            lo, size = k * cs, (cs if k < slots else rs)
            if m == 0:
                piece = own_ref[0, lo : lo + size, :]
            else:
                one, other = pairs[m - 1]
                piece = one[0, lo : lo + size, :] + other[0, lo : lo + size, :]
            if k < slots:
                w_ref[k, pl.ds(row, cs), :] = piece
            else:
                r_ref[m * rs : (m + 1) * rs, :] = piece

    starts = [pl.multiple_of(pattern_ref[base + step, k] * bs, bs) for k in range(slots)]
    preact = jnp.dot(ra_ref[...], r_ref[...], preferred_element_type=F32)
    for k in range(slots):
        preact += jnp.dot(x_ref[:, pl.ds(starts[k], bs)], w_ref[k], preferred_element_type=F32)
    cdf = 0.5 * (1.0 + lax.erf(preact * SQRT_HALF))
    hid_ref[...] = (preact * cdf).astype(BF16)
    slope = cdf + preact * jnp.exp(-0.5 * preact * preact) * INV_ROOT_TWO_PI
    grad = (cot_ref[...].astype(F32) * slope).astype(BF16)

    for k in range(slots):
        bt_ref[k] = jnp.dot(xt_ref[pl.ds(starts[k], bs), :], grad, preferred_element_type=F32).astype(BF16)
    right_term = jnp.dot(rat_ref[...], grad, preferred_element_type=F32).astype(BF16)
    for r in range(n):
        row = pl.multiple_of(lax.rem(me + r, n) * cs, cs)
        m = (n - r) % n
        for k in range(slots):
            term_refs[r][0, k * cs : (k + 1) * cs, :] = bt_ref[k, pl.ds(row, cs), :]
        term_refs[r][0, slots * cs :, :] = right_term[m * rs : (m + 1) * rs, :]
    across = (((1,), (1,)), ((), ()))
    for k in range(slots):
        acc_ref[:, pl.ds(starts[k], bs)] += lax.dot_general(grad, w_ref[k], across, preferred_element_type=F32)
    acc_ref[:, width:] += lax.dot_general(grad, r_ref[...], across, preferred_element_type=F32)


def run_chunk(n, slots, bs, base, cj, where, pattern, x, xt, ra, rat, cot, own, pairs, carried):
    tok = x.shape[0]
    rank = ra.shape[1]
    rows = own.shape[1]
    first = carried is None

    def whole(a):
        return pl.BlockSpec(a.shape, lambda i, *_: (0, 0))

    cols = pl.BlockSpec((tok, bs), lambda i, *_: (0, base + i))
    pack = pl.BlockSpec((1, rows, bs), lambda i, *_: (i, 0, 0))
    pack_own = pl.BlockSpec((1, rows, bs), lambda i, *_: (base + i, 0, 0))
    ins = [x, xt, ra, rat, cot, own] + [a for p in pairs for a in p]
    specs = [whole(x), whole(xt), whole(ra), whole(rat), cols, pack_own] + [pack] * (2 * (n - 1))
    aliases = {}
    if not first:
        aliases = {2 + len(ins): 1, 3 + len(ins): 0}
        ins += list(carried)
        specs += [pl.BlockSpec(memory_space=pl.ANY)] * 2
    acc_shape = (tok, x.shape[1] + rank)
    madds = tok * bs * bs * slots * 3 + tok * rank * bs * 3
    out = pl.pallas_call(
        functools.partial(chunk_kernel, n, slots, bs, first, base),
        grid_spec=pltpu.PrefetchScalarGridSpec(
            num_scalar_prefetch=2,
            grid=(cj,),
            in_specs=specs,
            out_specs=[cols, pl.BlockSpec(acc_shape, lambda i, *_: (0, 0))] + [pack] * n,
            scratch_shapes=[
                pltpu.VMEM((slots, bs, bs), BF16),
                pltpu.VMEM((rank, bs), BF16),
                pltpu.VMEM((slots, bs, bs), BF16),
            ],
        ),
        out_shape=[jax.ShapeDtypeStruct(cot.shape, BF16), jax.ShapeDtypeStruct(acc_shape, F32)]
        + [jax.ShapeDtypeStruct((cj, rows, bs), BF16)] * n,
        input_output_aliases=aliases,
        compiler_params=pltpu.CompilerParams(vmem_limit_bytes=60 * 1024 * 1024),
        cost_estimate=pl.CostEstimate(flops=2 * madds * cj, bytes_accessed=50_000_000, transcendentals=0),
    )(where, pattern, *ins)
    return out[0], out[1], out[2:]


def per_device(tokens, pattern, blocks, left_factor, right_factor, cotangent):
    n = lax.axis_size("dp")
    local_cols, slots, cs, bs = blocks.shape
    rs = right_factor.shape[0]
    rw = left_factor.shape[1]
    cj = local_cols // CHUNKS
    me = lax.axis_index("dp").astype(jnp.int32).reshape(1)
    local_pattern = lax.dynamic_slice_in_dim(pattern, lax.axis_index("tensor") * local_cols, local_cols, 0)

    left_pairs = line_gather(left_factor, n)
    packed = jnp.concatenate(
        [blocks.reshape(local_cols, slots * cs, bs), right_factor.reshape(rs, local_cols, bs).transpose(1, 0, 2)], axis=1
    )
    gathered = [line_gather(packed[c * cj : (c + 1) * cj], n) for c in range(CHUNKS)]

    x = lax.all_gather(tokens, "tensor", axis=1, tiled=True)
    xt = x.T
    left_rot = jnp.concatenate([left_factor] + [a + b for a, b in left_pairs], axis=1)
    rank_acts = lax.psum(jnp.dot(tokens, left_rot, preferred_element_type=F32), "tensor").astype(BF16)
    rank_acts_t = rank_acts.T

    carried = None
    sums = []
    for c in range(CHUNKS):
        hidden, acc, terms = run_chunk(
            n, slots, bs, c * cj, cj, me, local_pattern, x, xt, rank_acts, rank_acts_t, cotangent, packed, gathered[c], carried
        )
        carried = (acc, hidden)
        sums.append(line_scatter(list(terms), n))

    width = x.shape[1]
    rank_grad = lax.psum(acc[:, width:].astype(BF16), "tensor")
    token_part = lax.psum_scatter(acc[:, :width].astype(BF16), "tensor", scatter_dimension=1, tiled=True).astype(F32)
    left_term = lax.dot_general(tokens, rank_grad, (((0,), (0,)), ((), ())), preferred_element_type=F32).astype(BF16)
    left_terms = [left_term[:, ((n - r) % n) * rw : ((n - r) % n + 1) * rw] for r in range(n)]
    left_grad = line_scatter(left_terms, n)
    token_grad = token_part + lax.dot_general(
        rank_grad, left_rot, (((1,), (1,)), ((), ())), preferred_element_type=F32
    )
    block_grad = jnp.concatenate([s[:, : slots * cs].reshape(cj, slots, cs, bs) for s in sums], axis=0)
    right_grad = jnp.concatenate([s[:, slots * cs :].transpose(1, 0, 2).reshape(rs, cj * bs) for s in sums], axis=1)
    return (hidden, token_grad, block_grad, left_grad, right_grad)


def solution(mesh):
    placed = (
        P(("pipe", "dp"), "tensor"),
        P("pipe", None),
        P(("pipe", "tensor"), None, "dp", None),
        P(("pipe", "tensor"), "dp"),
        P(("pipe", "dp"), "tensor"),
        P(("pipe", "dp"), "tensor"),
    )
    return jax.shard_map(
        per_device,
        mesh=mesh,
        in_specs=placed,
        out_specs=(
            P(("pipe", "dp"), "tensor"),
            P(("pipe", "dp"), "tensor"),
            P(("pipe", "tensor"), None, "dp", None),
            P(("pipe", "tensor"), "dp"),
            P(("pipe", "dp"), "tensor"),
        ),
        check_vma=False,
    )
```

time: 939 us -> 788 us (0.84)
  waiting for transfers between devices: 654 us -> 388 us
  starting transfers between devices: 0.8 us -> 161 us
  Pallas kernels: 0 us -> 104 us
  matrix products: 91.4 us -> 9.39 us
  other arithmetic: 104 us -> 45.1 us
  local copies, waits for them, and re-layouts: 72.6 us -> 39.8 us
  blocking collectives: 0 us -> 20.4 us
    all_gather x5 -> x1, waiting for transfers between devices: 375 us -> 0.01 us  [per_device(): x = lax.all_gather(tokens, 'tensor', axis=1, tiled=True)]
    ppermute x0 -> x60, waiting for transfers between devices: none -> 362 us  [the longest x15 172 us: line_scatter(): got_left = lax.ppermute(to_right, 'dp', right_pairs)]
    reduce_scatter x4 -> x1, waiting for transfers between devices: 246 us -> 0.01 us  [per_device(): lax.psum_scatter(acc[:, :width].astype(BF16), 'tensor', scatter_dimension...]
    ppermute x0 -> x60, starting transfers between devices: none -> 161 us  [the longest x15 89.2 us: line_scatter(): got_left = lax.ppermute(to_right, 'dp', right_pairs)]
    pallas_call x0 -> x4, Pallas kernels: none -> 104 us  [run_chunk(): pl.pallas_call(functools.partial(chunk_kernel, n, slots, bs, first, base)...]
    scatter-add x1 -> x0, other arithmetic: 90.2 us -> none  [per_device(): placed = jnp.zeros((tok_rows, block_count, block_size), jnp.float32).at[:...]
    dot_general x8 -> x2, matrix products: 87.3 us -> 6.96 us  [the longest x1 4.76 us: per_device(): lax.dot_general(rank_grad, left_rot, (((1,), (1,)), ((), ())), preferred_...]
    gather x2 -> x0, local copies, waits for them, and re-layouts: 37.6 us -> none  [per_device(): jnp.take(full_tokens.reshape(tok_rows, block_count, block_size), local_pa...]
  transfers between devices with their start and end apart: 10 -> 63, of which waited for: 8 -> 25; matrix products, arithmetic and copies ran while one was open for 26% -> 9% of each run, Pallas kernels for 0% -> 10%
where the time goes in v1:
time: 788 us; the launch traced here: 783 us
  waiting for transfers between devices  388 us (49%)
  starting transfers between devices  161 us (20%)
  Pallas kernels  104 us (13%)
  other arithmetic  45.1 us (6%)
  local copies, waits for them, and re-layouts  39.8 us (5%)
  blocking collectives  20.4 us (3%)
  between operations  14.9 us (2%)
  matrix products  9.39 us (1%)
    ppermute x15, waiting for transfers between devices, line_scatter(): got_left = lax.ppermute(to_right, 'dp', right_pairs)  172 us
    ppermute x15, waiting for transfers between devices, line_gather(): lax.ppermute(own if m == 1 else from_right[m - 1], 'dp', left_pairs)  141 us
    pallas_call x4, Pallas kernels, run_chunk(): pl.pallas_call(functools.partial(chunk_kernel, n, slots, bs, first, base)...  104 us
    ppermute x15, starting transfers between devices, line_scatter(): got_left = lax.ppermute(to_right, 'dp', right_pairs)  89.2 us
    ppermute x15, waiting for transfers between devices, line_gather(): lax.ppermute(own if m == 1 else from_left[m - 1], 'dp', right_pairs)  48.2 us
    ppermute x15, starting transfers between devices, line_gather(): lax.ppermute(own if m == 1 else from_left[m - 1], 'dp', right_pairs)  36.9 us
    psum x1, waiting for transfers between devices, per_device(): rank_grad = lax.psum(acc[:, width:].astype(BF16), 'tensor')  26.5 us
    psum x1, blocking collectives, per_device(): lax.psum(jnp.dot(tokens, left_rot, preferred_element_type=F32), 'tensor')  20.4 us
  transfers between devices with their start and end apart: 63, of which 25 were waited for; matrix products, arithmetic and copies ran while one was open for 9% of the time, Pallas kernels for 10%

profile of v1, /device:TPU:0, one launch (start us, length us, event | category | flops | bytes accessed | tf_op | source)
XLA Modules:
  0.0 782.6 jit_solution(4751347828447301958)
XLA Ops:
  11.5 6.4 collective-permute-start
  25.5 4.6 collective-permute-start.24
  33.4 50.9 %collective-permute-done.2 = bf16[2048,128]{1,0:T(8,128)(2,1)S(1)} collective-permute-done((bf16[2048,128]{1,0:T(8,128)(2,1)}, bf16[2048,128]{1,0:T(8,128)(2,1)S(1)}, u32[]{:S(2)}, u32[]{:S(2)}) %collective-permute-start.2) | collective-permute-done | bytes 524320 | tf_op jit(solution)/shard_map/ppermute | solution.py:23
  89.2 5.6 collective-permute-start.12
  98.3 13.1 %collective-permute-done.18.rest_1_ = bf16[4,512,256]{2,1,0:T(8,128)(2,1)S(1)} collective-permute-done((bf16[4,512,256]{2,1,0:T(8,128)(2,1)S(1)}, bf16[4,512,256]{2,1,0:T(8,128)(2,1)S(1)}, u32[]{:S(2)}, u32[]{:S(2)}) %collective-permute-start.18) | collective-permute-done | bytes 1048608 | tf_op jit(solution)/shard_map/ppermute | solution.py:22
  117.3 16.6 %collective-permute-done.12.rest_1_ = bf16[4,512,256]{2,1,0:T(8,128)(2,1)} collective-permute-done((bf16[4,512,256]{2,1,0:T(8,128)(2,1)S(1)}, bf16[4,512,256]{2,1,0:T(8,128)(2,1)}, u32[]{:S(2)}, u32[]{:S(2)}) %collective-permute-start.12) | collective-permute-done | bytes 1048608 | tf_op jit(solution)/shard_map/ppermute | solution.py:22
  135.5 18.5 %collective-permute-done.6.rest_1_ = bf16[4,512,256]{2,1,0:T(8,128)(2,1)} collective-permute-done((bf16[4,512,256]{2,1,0:T(8,128)(2,1)S(1)}, bf16[4,512,256]{2,1,0:T(8,128)(2,1)}, u32[]{:S(2)}, u32[]{:S(2)}) %collective-permute-start.6) | collective-permute-done | bytes 1048608 | tf_op jit(solution)/shard_map/ppermute | solution.py:22
  159.0 13.2 %collective-permute-done.26.rest_4_ = bf16[4,512,256]{2,1,0:T(8,128)(2,1)} collective-permute-done((bf16[4,512,256]{2,1,0:T(8,128)(2,1)S(1)}, bf16[4,512,256]{2,1,0:T(8,128)(2,1)}, u32[]{:S(2)}, u32[]{:S(2)}) %collective-permute-start.26) | collective-permute-done | bytes 1048608 | tf_op jit(solution)/shard_map/ppermute | solution.py:23
  175.4 19.1 %collective-permute-done.20.rest_4_ = bf16[4,512,256]{2,1,0:T(8,128)(2,1)S(1)} collective-permute-done((bf16[4,512,256]{2,1,0:T(8,128)(2,1)S(1)}, bf16[4,512,256]{2,1,0:T(8,128)(2,1)S(1)}, u32[]{:S(2)}, u32[]{:S(2)}) %collective-permute-start.20) | collective-permute-done | bytes 1048608 | tf_op jit(solution)/shard_map/ppermute | solution.py:23
  204.8 9.7 %collective-permute-done.14.rest_4_ = bf16[4,512,256]{2,1,0:T(8,128)(2,1)} collective-permute-done((bf16[4,512,256]{2,1,0:T(8,128)(2,1)}, bf16[4,512,256]{2,1,0:T(8,128)(2,1)}, u32[]{:S(2)}, u32[]{:S(2)}) %collective-permute-start.14) | collective-permute-done | bytes 1048608 | tf_op jit(solution)/shard_map/ppermute | solution.py:23
  221.3 24.0 %collective-permute-done.8.rest_4_ = bf16[4,512,256]{2,1,0:T(8,128)(2,1)} collective-permute-done((bf16[4,512,256]{2,1,0:T(8,128)(2,1)}, bf16[4,512,256]{2,1,0:T(8,128)(2,1)}, u32[]{:S(2)}, u32[]{:S(2)}) %collective-permute-start.8) | collective-permute-done | bytes 1048608 | tf_op jit(solution)/shard_map/ppermute | solution.py:23
  246.6 21.2 %collective-permute-done.27.rest_2_ = bf16[4,512,256]{2,1,0:T(8,128)(2,1)} collective-permute-done((bf16[4,512,256]{2,1,0:T(8,128)(2,1)}, bf16[4,512,256]{2,1,0:T(8,128)(2,1)}, u32[]{:S(2)}, u32[]{:S(2)}) %collective-permute-start.27) | collective-permute-done | bytes 1048608 | tf_op jit(solution)/shard_map/ppermute | solution.py:23
  269.5 20.4 %all-reduce.4 = bf16[384,512]{0,1:T(8,128)(2,1)S(1)} all-reduce(f32[384,512]{0,1:T(8,128)} %convolution_bitcast_fusion), channel_id=1, replica_groups=mesh['pipe'=2,'dp'=4,'tensor'=4] {'tensor'}, use_global_device_ids=true, to_apply=%region_0.0 | all-reduce | flops 196608 | bytes 1179648 | tf_op jit(solution)/shard_map/psum | solution.py:161
  290.9 8.6 %copy.38.x_ref = bf16[384,8192]{1,0:T(8,128)(2,1)} copy(bf16[384,8192]{0,1:T(8,128)(2,1)} %all-gather.2.cloned.1.call-done) | data formatting | bytes 12582912 | tf_op jit(solution)/shard_map/all_gather | solution.py:158
  302.6 22.9 %shard_map.101 = (bf16[384,4096]{1,0:T(8,128)(2,1)}, f32[384,8704]{1,0:T(8,128)}, bf16[4,512,256]{2,1,0:T(8,128)(2,1)}, bf16[4,512,256]{2,1,0:T(8,128)(2,1)}, bf...) custom-call(s32[1]{0:T(128)} %bitcast.where_ref, s32[16,6]{1,0:T(8,128)} %copy.46.pattern_ref, ...), custom_call_target="tpu_custom_call" | custom-call | flops 4831838208 | bytes 50000000 | tf_op jit(solution)/shard_map/pallas_call | solution.py:121
  325.5 27.1 %shard_map.102 = (bf16[384,4096]{1,0:T(8,128)(2,1)}, f32[384,8704]{1,0:T(8,128)}, bf16[4,512,256]{2,1,0:T(8,128)(2,1)}, bf16[4,512,256]{2,1,0:T(8,128)(2,1)}, bf...) custom-call(s32[1]{0:T(128)} %bitcast.where_ref, ...), custom_call_target="tpu_custom_call", output_to_operand_aliasing={{1}: (14, {}), {0}: (15, {})} | custom-call | flops 4831838208 | bytes 50000000 | tf_op jit(solution)/shard_map/pallas_call | solution.py:121
  352.6 27.0 %shard_map.103 = (bf16[384,4096]{1,0:T(8,128)(2,1)}, f32[384,8704]{1,0:T(8,128)}, bf16[4,512,256]{2,1,0:T(8,128)(2,1)}, bf16[4,512,256]{2,1,0:T(8,128)(2,1)}, bf...) custom-call(s32[1]{0:T(128)} %bitcast.where_ref, ...), custom_call_target="tpu_custom_call", output_to_operand_aliasing={{1}: (14, {}), {0}: (15, {})} | custom-call | flops 4831838208 | bytes 50000000 | tf_op jit(solution)/shard_map/pallas_call | solution.py:121
  380.6 27.0 %shard_map.104 = (bf16[384,4096]{1,0:T(8,128)(2,1)}, f32[384,8704]{1,0:T(8,128)}, bf16[4,512,256]{2,1,0:T(8,128)(2,1)}, bf16[4,512,256]{2,1,0:T(8,128)(2,1)}, bf...) custom-call(s32[1]{0:T(128)} %bitcast.where_ref, ...), custom_call_target="tpu_custom_call", output_to_operand_aliasing={{1}: (14, {}), {0}: (15, {})} | custom-call | flops 4831838208 | bytes 50000000 | tf_op jit(solution)/shard_map/pallas_call | solution.py:121
  407.6 8.2 %convert.4 = bf16[384,8704]{1,0:T(8,128)(2,1)} convert(f32[384,8704]{1,0:T(8,128)} %get-tuple-element.36) | non-fusion elementwise | flops 3342336 | bytes 20054016 | tf_op jit(solution)/shard_map/convert.1
  417.6 6.1 slice.82
  423.7 26.5 %all-reduce.3.cloned.1.call-done = bf16[384,512]{1,0:T(8,128)(2,1)} async-done(((bf16[384,512]{1,0:T(8,128)(2,1)}), bf16[384,512]{1,0:T(8,128)(2,1)}) %all-reduce.3.cloned.1.call-update) | async-done | bytes 393232 | tf_op jit(solution)/shard_map/psum | solution.py:174
  461.0 7.9 %collective-permute-done.54 = bf16[2048,128]{0,1:T(8,128)(2,1)S(1)} collective-permute-done((bf16[2048,128]{0,1:T(8,128)(2,1)S(1)}, bf16[2048,128]{0,1:T(8,128)(2,1)S(1)}, u32[]{:S(2)}, u32[]{:S(2)}) %collective-permute-start.54) | collective-permute-done | bytes 524320 | tf_op jit(solution)/shard_map/ppermute | solution.py:34
  474.2 17.2 %collective-permute-done.30 = bf16[4,512,256]{2,1,0:T(8,128)(2,1)S(1)} collective-permute-done((bf16[4,512,256]{2,1,0:T(8,128)(2,1)S(1)}, bf16[4,512,256]{2,1,0:T(8,128)(2,1)S(1)}, u32[]{:S(2)}, u32[]{:S(2)}) %collective-permute-start.30) | collective-permute-done | bytes 1048608 | tf_op jit(solution)/shard_map/ppermute | solution.py:34
  491.4 4.4 collective-permute-start.42
  496.6 17.3 %collective-permute-done.36 = bf16[4,512,256]{2,1,0:T(8,128)(2,1)S(1)} collective-permute-done((bf16[4,512,256]{2,1,0:T(8,128)(2,1)S(1)}, bf16[4,512,256]{2,1,0:T(8,128)(2,1)S(1)}, u32[]{:S(2)}, u32[]{:S(2)}) %collective-permute-start.36) | collective-permute-done | bytes 1048608 | tf_op jit(solution)/shard_map/ppermute | solution.py:34
  513.8 4.4 collective-permute-start.48
  518.3 6.8 collective-permute-done.55
  527.8 13.8 %collective-permute-start.31 = (bf16[4,512,256]{2,1,0:T(8,128)(2,1)S(1)}, bf16[4,512,256]{2,1,0:T(8,128)(2,1)S(1)}, u32[]{:S(2)}, u32[]{:S(2)}) collective-permute-start(bf16[4,512,256]{2,1,0:T(8,128)(2,1)S(1)} %get-tuple-element.73), channel_id=1, source_target_pairs={{0,4},{4,8},{1,5},{5,9},{2,6},{6,10},{3,7},{7,11},{16,20},{20,24},... | collective-permute-start | bytes 3145736 | tf_op jit(solution)/shard_map/ppermute | solution.py:34
  541.6 5.9 collective-permute-done.42
  548.3 8.2 %collective-permute-start.56 = (bf16[2048,128]{0,1:T(8,128)(2,1)S(1)}, bf16[2048,128]{0,1:T(8,128)(2,1)S(1)}, u32[]{:S(2)}, u32[]{:S(2)}) collective-permute-start(bf16[2048,128]{0,1:T(8,128)(2,1)S(1)} %get-tuple-element.67), channel_id=1, source_target_pairs={{0,4},{4,8},{8,12},{1,5},{5,9},{9,13},{2,6},{6,10},{10,14},{3,7},{... | collective-permute-start | bytes 1572872 | tf_op jit(solution)/shard_map/ppermute | solution.py:34
  556.5 13.5 %collective-permute-done.48 = bf16[4,512,256]{2,1,0:T(8,128)(2,1)S(1)} collective-permute-done((bf16[4,512,256]{2,1,0:T(8,128)(2,1)S(1)}, bf16[4,512,256]{2,1,0:T(8,128)(2,1)S(1)}, u32[]{:S(2)}, u32[]{:S(2)}) %collective-permute-start.48) | collective-permute-done | bytes 1048608 | tf_op jit(solution)/shard_map/ppermute | solution.py:34
  572.7 5.2 collective-permute-start.37
  577.9 25.8 %collective-permute-done.56 = bf16[2048,128]{0,1:T(8,128)(2,1)S(1)} collective-permute-done((bf16[2048,128]{0,1:T(8,128)(2,1)S(1)}, bf16[2048,128]{0,1:T(8,128)(2,1)S(1)}, u32[]{:S(2)}, u32[]{:S(2)}) %collective-permute-start.56) | collective-permute-done | bytes 524320 | tf_op jit(solution)/shard_map/ppermute | solution.py:34
  604.5 5.0 collective-permute-start.43
  611.4 6.6 collective-permute-start.49
  619.2 7.0 collective-permute-done.37
  629.1 8.0 %collective-permute-start.32 = (bf16[4,512,256]{2,1,0:T(8,128)(2,1)}, bf16[4,512,256]{2,1,0:T(8,128)(2,1)}, u32[]{:S(2)}, u32[]{:S(2)}) collective-permute-start(bf16[4,512,256]{2,1,0:T(8,128)(2,1)} %add.117), channel_id=1, source_target_pairs={{0,4},{4,8},{8,12},{1,5},{5,9},{9,13},{2,6},{6,10},{10,14},{3,7},{... | collective-permute-start | bytes 3145736 | tf_op jit(solution)/shard_map/ppermute | solution.py:34
  637.1 11.6 %collective-permute-done.43 = bf16[4,512,256]{2,1,0:T(8,128)(2,1)S(1)} collective-permute-done((bf16[4,512,256]{2,1,0:T(8,128)(2,1)S(1)}, bf16[4,512,256]{2,1,0:T(8,128)(2,1)S(1)}, u32[]{:S(2)}, u32[]{:S(2)}) %collective-permute-start.43) | collective-permute-done | bytes 1048608 | tf_op jit(solution)/shard_map/ppermute | solution.py:34
  652.5 7.1 collective-permute-start.38
  659.5 11.6 %collective-permute-done.49 = bf16[4,512,256]{2,1,0:T(8,128)(2,1)S(1)} collective-permute-done((bf16[4,512,256]{2,1,0:T(8,128)(2,1)S(1)}, bf16[4,512,256]{2,1,0:T(8,128)(2,1)S(1)}, u32[]{:S(2)}, u32[]{:S(2)}) %collective-permute-start.49) | collective-permute-done | bytes 1048608 | tf_op jit(solution)/shard_map/ppermute | solution.py:34
  679.8 6.1 collective-permute-start.44
  688.3 5.4 collective-permute-done.32
  695.0 9.6 %collective-permute-start.50 = (bf16[4,512,256]{2,1,0:T(8,128)(2,1)}, bf16[4,512,256]{2,1,0:T(8,128)(2,1)}, u32[]{:S(2)}, u32[]{:S(2)}) collective-permute-start(bf16[4,512,256]{2,1,0:T(8,128)(2,1)} %add.135), channel_id=1, source_target_pairs={{0,4},{4,8},{8,12},{1,5},{5,9},{9,13},{2,6},{6,10},{10,14},{3,7},{... | collective-permute-start | bytes 3145736 | tf_op jit(solution)/shard_map/ppermute | solution.py:34
  708.0 8.2 %collective-permute-done.38 = bf16[4,512,256]{2,1,0:T(8,128)(2,1)} collective-permute-done((bf16[4,512,256]{2,1,0:T(8,128)(2,1)}, bf16[4,512,256]{2,1,0:T(8,128)(2,1)}, u32[]{:S(2)}, u32[]{:S(2)}) %collective-permute-start.38) | collective-permute-done | bytes 1048608 | tf_op jit(solution)/shard_map/ppermute | solution.py:34
  721.5 17.2 %collective-permute-done.44 = bf16[4,512,256]{2,1,0:T(8,128)(2,1)} collective-permute-done((bf16[4,512,256]{2,1,0:T(8,128)(2,1)}, bf16[4,512,256]{2,1,0:T(8,128)(2,1)}, u32[]{:S(2)}, u32[]{:S(2)}) %collective-permute-start.44) | collective-permute-done | bytes 1048608 | tf_op jit(solution)/shard_map/ppermute | solution.py:34
  742.1 16.7 %collective-permute-done.50 = bf16[4,512,256]{2,1,0:T(8,128)(2,1)} collective-permute-done((bf16[4,512,256]{2,1,0:T(8,128)(2,1)}, bf16[4,512,256]{2,1,0:T(8,128)(2,1)}, u32[]{:S(2)}, u32[]{:S(2)}) %collective-permute-start.50) | collective-permute-done | bytes 1048608 | tf_op jit(solution)/shard_map/ppermute | solution.py:34
  766.8 4.5 pad_maximum_fusion.1
  771.3 4.8 convert_add_fusion
  (240 shorter events, 131.4 us)
Async XLA Ops:
  7.2 283.7 %all-gather.2.cloned.1.call-start = ((), (), s32[]{:S(2)}) async-start(), calls=%async_computation.1 | async-start | bytes 7864320 | tf_op jit(solution)/shard_map/all_gather | solution.py:158
  9.8 440.4 %all-reduce.3.cloned.1.call-start = ((), (), s32[]{:S(2)}) async-start(), calls=%async_computation.3 | async-start | bytes 786432 | tf_op jit(solution)/shard_map/psum | solution.py:174
  24.2 65.0 %collective-permute-start.25 = (bf16[4,512,256]{2,1,0:T(8,128)(2,1)S(1)}, bf16[4,512,256]{2,1,0:T(8,128)(2,1)S(1)}, u32[]{:S(2)}, u32[]{:S(2)}) collective-permute-start(bf16[4,512,256]{2,1,0:T(8,128)(2,1)S(1)} %get-tuple-element.63), channel_id=1, source_target_pairs={{4,0},{8,4},{12,8},{5,1},{9,5},{13,9},{6,2},{10,6},{14,10},{7,3},{... | collective-permute-start | bytes 3145736 | tf_op jit(solution)/shard_map/ppermute | solution.py:23
  25.5 69.3 %collective-permute-start.24 = (bf16[4,512,256]{2,1,0:T(8,128)(2,1)S(1)}, bf16[4,512,256]{2,1,0:T(8,128)(2,1)S(1)}, u32[]{:S(2)}, u32[]{:S(2)}) collective-permute-start(bf16[4,512,256]{2,1,0:T(8,128)(2,1)S(1)} %get-tuple-element.63), channel_id=1, source_target_pairs={{0,4},{4,8},{8,12},{1,5},{5,9},{9,13},{2,6},{6,10},{10,14},{3,7},{... | collective-permute-start | bytes 3145736 | tf_op jit(solution)/shard_map/ppermute | solution.py:22
  30.1 66.9 %collective-permute-start.19 = (bf16[4,512,256]{2,1,0:T(8,128)(2,1)S(1)}, bf16[4,512,256]{2,1,0:T(8,128)(2,1)S(1)}, u32[]{:S(2)}, u32[]{:S(2)}) collective-permute-start(bf16[4,512,256]{2,1,0:T(8,128)(2,1)S(1)} %get-tuple-element.66), channel_id=1, source_target_pairs={{4,0},{8,4},{12,8},{5,1},{9,5},{13,9},{6,2},{10,6},{14,10},{7,3},{... | collective-permute-start | bytes 3145736 | tf_op jit(solution)/shard_map/ppermute | solution.py:23
  31.4 53.0 %collective-permute-start.2 = (bf16[2048,128]{1,0:T(8,128)(2,1)}, bf16[2048,128]{1,0:T(8,128)(2,1)S(1)}, u32[]{:S(2)}, u32[]{:S(2)}) collective-permute-start(bf16[2048,128]{1,0:T(8,128)(2,1)} %collective-permute-done.1), channel_id=1, source_target_pairs={{4,0},{8,4},{5,1},{9,5},{6,2},{10,6},{7,3},{11,7},{20,16},{24,20},... | collective-permute-start | bytes 1572872 | tf_op jit(solution)/shard_map/ppermute | solution.py:23
  32.7 55.1 %collective-permute-start.4 = (bf16[2048,128]{1,0:T(8,128)(2,1)}, bf16[2048,128]{1,0:T(8,128)(2,1)S(1)}, u32[]{:S(2)}, u32[]{:S(2)}) collective-permute-start(bf16[2048,128]{1,0:T(8,128)(2,1)} %collective-permute-done), channel_id=1, source_target_pairs={{4,8},{8,12},{5,9},{9,13},{6,10},{10,14},{7,11},{11,15},{20,24},{2... | collective-permute-start | bytes 1572872 | tf_op jit(solution)/shard_map/ppermute | solution.py:22
  89.2 44.7 %collective-permute-start.12 = (bf16[4,512,256]{2,1,0:T(8,128)(2,1)S(1)}, bf16[4,512,256]{2,1,0:T(8,128)(2,1)}, u32[]{:S(2)}, u32[]{:S(2)}) collective-permute-start(bf16[4,512,256]{2,1,0:T(8,128)(2,1)S(1)} %get-tuple-element.65), channel_id=1, source_target_pairs={{0,4},{4,8},{8,12},{1,5},{5,9},{9,13},{2,6},{6,10},{10,14},{3,7},{... | collective-permute-start | bytes 3145736 | tf_op jit(solution)/shard_map/ppermute | solution.py:22
  94.8 59.2 %collective-permute-start.6 = (bf16[4,512,256]{2,1,0:T(8,128)(2,1)S(1)}, bf16[4,512,256]{2,1,0:T(8,128)(2,1)}, u32[]{:S(2)}, u32[]{:S(2)}) collective-permute-start(bf16[4,512,256]{2,1,0:T(8,128)(2,1)S(1)} %get-tuple-element.64), channel_id=1, source_target_pairs={{0,4},{4,8},{8,12},{1,5},{5,9},{9,13},{2,6},{6,10},{10,14},{3,7},{... | collective-permute-start | bytes 3145736 | tf_op jit(solution)/shard_map/ppermute | solution.py:22
  97.0 58.2 %collective-permute-start.7 = (bf16[4,512,256]{2,1,0:T(8,128)(2,1)S(1)}, bf16[4,512,256]{2,1,0:T(8,128)(2,1)}, u32[]{:S(2)}, u32[]{:S(2)}) collective-permute-start(bf16[4,512,256]{2,1,0:T(8,128)(2,1)S(1)} %get-tuple-element.64), channel_id=1, source_target_pairs={{4,0},{8,4},{12,8},{5,1},{9,5},{13,9},{6,2},{10,6},{14,10},{7,3},{... | collective-permute-start | bytes 3145736 | tf_op jit(solution)/shard_map/ppermute | solution.py:23
  111.4 45.6 %collective-permute-start.3 = (bf16[2048,128]{1,0:T(8,128)(2,1)S(1)}, bf16[2048,128]{1,0:T(8,128)(2,1)S(1)}, u32[]{:S(2)}, u32[]{:S(2)}) collective-permute-start(bf16[2048,128]{1,0:T(8,128)(2,1)S(1)} %collective-permute-done.2), channel_id=1, source_target_pairs={{4,0},{5,1},{6,2},{7,3},{20,16},{21,17},{22,18},{23,19}} | collective-permute-start | bytes 1572872 | tf_op jit(solution)/shard_map/ppermute | solution.py:23
  116.0 56.2 %collective-permute-start.26 = (bf16[4,512,256]{2,1,0:T(8,128)(2,1)S(1)}, bf16[4,512,256]{2,1,0:T(8,128)(2,1)}, u32[]{:S(2)}, u32[]{:S(2)}) collective-permute-start(bf16[4,512,256]{2,1,0:T(8,128)(2,1)S(1)} %collective-permute-done.25.rest_6_), channel_id=1, source_target_pairs={{4,0},{8,4},{5,1},{9,5},{6,2},{10,6},{7,3},{11,7},{20,16},{24,20},... | collective-permute-start | bytes 3145736 | tf_op jit(solution)/shard_map/ppermute | solution.py:23
  157.7 56.8 %collective-permute-start.14 = (bf16[4,512,256]{2,1,0:T(8,128)(2,1)}, bf16[4,512,256]{2,1,0:T(8,128)(2,1)}, u32[]{:S(2)}, u32[]{:S(2)}) collective-permute-start(bf16[4,512,256]{2,1,0:T(8,128)(2,1)} %collective-permute-done.13.rest_6_), channel_id=1, source_target_pairs={{4,0},{8,4},{5,1},{9,5},{6,2},{10,6},{7,3},{11,7},{20,16},{24,20},... | collective-permute-start | bytes 3145736 | tf_op jit(solution)/shard_map/ppermute | solution.py:23
  172.2 43.9 %collective-permute-start.16 = (bf16[4,512,256]{2,1,0:T(8,128)(2,1)}, bf16[4,512,256]{2,1,0:T(8,128)(2,1)}, u32[]{:S(2)}, u32[]{:S(2)}) collective-permute-start(bf16[4,512,256]{2,1,0:T(8,128)(2,1)} %collective-permute-done.12.rest_1_), channel_id=1, source_target_pairs={{4,8},{8,12},{5,9},{9,13},{6,10},{10,14},{7,11},{11,15},{20,24},{2... | collective-permute-start | bytes 3145736 | tf_op jit(solution)/shard_map/ppermute | solution.py:22
  173.8 45.8 %collective-permute-start.10 = (bf16[4,512,256]{2,1,0:T(8,128)(2,1)}, bf16[4,512,256]{2,1,0:T(8,128)(2,1)}, u32[]{:S(2)}, u32[]{:S(2)}) collective-permute-start(bf16[4,512,256]{2,1,0:T(8,128)(2,1)} %collective-permute-done.6.rest_1_), channel_id=1, source_target_pairs={{4,8},{8,12},{5,9},{9,13},{6,10},{10,14},{7,11},{11,15},{20,24},{2... | collective-permute-start | bytes 3145736 | tf_op jit(solution)/shard_map/ppermute | solution.py:22
  194.5 50.8 %collective-permute-start.8 = (bf16[4,512,256]{2,1,0:T(8,128)(2,1)}, bf16[4,512,256]{2,1,0:T(8,128)(2,1)}, u32[]{:S(2)}, u32[]{:S(2)}) collective-permute-start(bf16[4,512,256]{2,1,0:T(8,128)(2,1)} %collective-permute-done.7.rest_6_), channel_id=1, source_target_pairs={{4,0},{8,4},{5,1},{9,5},{6,2},{10,6},{7,3},{11,7},{20,16},{24,20},... | collective-permute-start | bytes 3145736 | tf_op jit(solution)/shard_map/ppermute | solution.py:23
  195.9 71.9 %collective-permute-start.27 = (bf16[4,512,256]{2,1,0:T(8,128)(2,1)}, bf16[4,512,256]{2,1,0:T(8,128)(2,1)}, u32[]{:S(2)}, u32[]{:S(2)}) collective-permute-start(bf16[4,512,256]{2,1,0:T(8,128)(2,1)} %collective-permute-done.26.rest_4_), channel_id=1, source_target_pairs={{4,0},{5,1},{6,2},{7,3},{20,16},{21,17},{22,18},{23,19}} | collective-permute-start | bytes 3145736 | tf_op jit(solution)/shard_map/ppermute | solution.py:23
  214.5 85.0 %collective-permute-start.29 = (bf16[4,512,256]{2,1,0:T(8,128)(2,1)}, bf16[4,512,256]{2,1,0:T(8,128)(2,1)}, u32[]{:S(2)}, u32[]{:S(2)}) collective-permute-start(bf16[4,512,256]{2,1,0:T(8,128)(2,1)} %collective-permute-done.28.rest_3_), channel_id=1, source_target_pairs={{8,12},{9,13},{10,14},{11,15},{24,28},{25,29},{26,30},{27,31}} | collective-permute-start | bytes 3145736 | tf_op jit(solution)/shard_map/ppermute | solution.py:22
  216.1 85.1 %collective-permute-start.21 = (bf16[4,512,256]{2,1,0:T(8,128)(2,1)S(1)}, bf16[4,512,256]{2,1,0:T(8,128)(2,1)}, u32[]{:S(2)}, u32[]{:S(2)}) collective-permute-start(bf16[4,512,256]{2,1,0:T(8,128)(2,1)S(1)} %copy-done.29), channel_id=1, source_target_pairs={{4,0},{5,1},{6,2},{7,3},{20,16},{21,17},{22,18},{23,19}} | collective-permute-start | bytes 3145736 | tf_op jit(solution)/shard_map/ppermute | solution.py:23
  219.6 105.9 %collective-permute-start.23 = (bf16[4,512,256]{2,1,0:T(8,128)(2,1)}, bf16[4,512,256]{2,1,0:T(8,128)(2,1)}, u32[]{:S(2)}, u32[]{:S(2)}) collective-permute-start(bf16[4,512,256]{2,1,0:T(8,128)(2,1)} %collective-permute-done.22.rest_3_), channel_id=1, source_target_pairs={{8,12},{9,13},{10,14},{11,15},{24,28},{25,29},{26,30},{27,31}} | collective-permute-start | bytes 3145736 | tf_op jit(solution)/shard_map/ppermute | solution.py:22
  245.3 107.3 %collective-permute-start.15 = (bf16[4,512,256]{2,1,0:T(8,128)(2,1)}, bf16[4,512,256]{2,1,0:T(8,128)(2,1)}, u32[]{:S(2)}, u32[]{:S(2)}) collective-permute-start(bf16[4,512,256]{2,1,0:T(8,128)(2,1)} %collective-permute-done.14.rest_4_), channel_id=1, source_target_pairs={{4,0},{5,1},{6,2},{7,3},{20,16},{21,17},{22,18},{23,19}} | collective-permute-start | bytes 3145736 | tf_op jit(solution)/shard_map/ppermute | solution.py:23
  267.8 84.8 %collective-permute-start.17 = (bf16[4,512,256]{2,1,0:T(8,128)(2,1)}, bf16[4,512,256]{2,1,0:T(8,128)(2,1)}, u32[]{:S(2)}, u32[]{:S(2)}) collective-permute-start(bf16[4,512,256]{2,1,0:T(8,128)(2,1)} %collective-permute-done.16.rest_3_), channel_id=1, source_target_pairs={{8,12},{9,13},{10,14},{11,15},{24,28},{25,29},{26,30},{27,31}} | collective-permute-start | bytes 3145736 | tf_op jit(solution)/shard_map/ppermute | solution.py:22
  299.5 80.1 %collective-permute-start.11 = (bf16[4,512,256]{2,1,0:T(8,128)(2,1)}, bf16[4,512,256]{2,1,0:T(8,128)(2,1)}, u32[]{:S(2)}, u32[]{:S(2)}) collective-permute-start(bf16[4,512,256]{2,1,0:T(8,128)(2,1)} %collective-permute-done.10.rest_3_), channel_id=1, source_target_pairs={{8,12},{9,13},{10,14},{11,15},{24,28},{25,29},{26,30},{27,31}} | collective-permute-start | bytes 3145736 | tf_op jit(solution)/shard_map/ppermute | solution.py:22
  301.2 78.5 %collective-permute-start.9 = (bf16[4,512,256]{2,1,0:T(8,128)(2,1)}, bf16[4,512,256]{2,1,0:T(8,128)(2,1)S(1)}, u32[]{:S(2)}, u32[]{:S(2)}) collective-permute-start(bf16[4,512,256]{2,1,0:T(8,128)(2,1)} %collective-permute-done.8.rest_4_), channel_id=1, source_target_pairs={{4,0},{5,1},{6,2},{7,3},{20,16},{21,17},{22,18},{23,19}} | collective-permute-start | bytes 3145736 | tf_op jit(solution)/shard_map/ppermute | solution.py:23
  417.6 353.7 %reduce-scatter.2.cloned.1.call-start = ((), (), s32[]{:S(2)}) async-start(), calls=%async_computation.2 | async-start | bytes 7864320 | tf_op jit(solution)/shard_map/reduce_scatter | solution.py:175
  459.6 54.2 %collective-permute-start.36 = (bf16[4,512,256]{2,1,0:T(8,128)(2,1)S(1)}, bf16[4,512,256]{2,1,0:T(8,128)(2,1)S(1)}, u32[]{:S(2)}, u32[]{:S(2)}) collective-permute-start(bf16[4,512,256]{2,1,0:T(8,128)(2,1)S(1)} %copy-done.14), channel_id=1, source_target_pairs={{0,4},{1,5},{2,6},{3,7},{16,20},{17,21},{18,22},{19,23}} | collective-permute-start | bytes 3145736 | tf_op jit(solution)/shard_map/ppermute | solution.py:34
  469.0 56.1 %collective-permute-start.55 = (bf16[2048,128]{0,1:T(8,128)(2,1)S(1)}, bf16[2048,128]{0,1:T(8,128)(2,1)S(1)}, u32[]{:S(2)}, u32[]{:S(2)}) collective-permute-start(bf16[2048,128]{0,1:T(8,128)(2,1)S(1)} %get-tuple-element.69), channel_id=1, source_target_pairs={{0,4},{4,8},{1,5},{5,9},{2,6},{6,10},{3,7},{7,11},{16,20},{20,24},... | collective-permute-start | bytes 1572872 | tf_op jit(solution)/shard_map/ppermute | solution.py:34
  473.4 54.4 %collective-permute-start.39 = (bf16[4,512,256]{2,1,0:T(8,128)(2,1)S(1)}, bf16[4,512,256]{2,1,0:T(8,128)(2,1)S(1)}, u32[]{:S(2)}, u32[]{:S(2)}) collective-permute-start(bf16[4,512,256]{2,1,0:T(8,128)(2,1)S(1)} %copy-done.15), channel_id=1, source_target_pairs={{12,8},{13,9},{14,10},{15,11},{28,24},{29,25},{30,26},{31,27}} | collective-permute-start | bytes 3145736 | tf_op jit(solution)/shard_map/ppermute | solution.py:35
  491.4 56.2 %collective-permute-start.42 = (bf16[4,512,256]{2,1,0:T(8,128)(2,1)S(1)}, bf16[4,512,256]{2,1,0:T(8,128)(2,1)S(1)}, u32[]{:S(2)}, u32[]{:S(2)}) collective-permute-start(bf16[4,512,256]{2,1,0:T(8,128)(2,1)S(1)} %copy-done.10), channel_id=1, source_target_pairs={{0,4},{1,5},{2,6},{3,7},{16,20},{17,21},{18,22},{19,23}} | collective-permute-start | bytes 3145736 | tf_op jit(solution)/shard_map/ppermute | solution.py:34
  495.8 52.4 %collective-permute-start.45 = (bf16[4,512,256]{2,1,0:T(8,128)(2,1)S(1)}, bf16[4,512,256]{2,1,0:T(8,128)(2,1)S(1)}, u32[]{:S(2)}, u32[]{:S(2)}) collective-permute-start(bf16[4,512,256]{2,1,0:T(8,128)(2,1)S(1)} %copy-done.11), channel_id=1, source_target_pairs={{12,8},{13,9},{14,10},{15,11},{28,24},{29,25},{30,26},{31,27}} | collective-permute-start | bytes 3145736 | tf_op jit(solution)/shard_map/ppermute | solution.py:35
  513.8 56.2 %collective-permute-start.48 = (bf16[4,512,256]{2,1,0:T(8,128)(2,1)S(1)}, bf16[4,512,256]{2,1,0:T(8,128)(2,1)S(1)}, u32[]{:S(2)}, u32[]{:S(2)}) collective-permute-start(bf16[4,512,256]{2,1,0:T(8,128)(2,1)S(1)} %copy-done.12), channel_id=1, source_target_pairs={{0,4},{1,5},{2,6},{3,7},{16,20},{17,21},{18,22},{19,23}} | collective-permute-start | bytes 3145736 | tf_op jit(solution)/shard_map/ppermute | solution.py:34
  527.0 45.7 %collective-permute-start.51 = (bf16[4,512,256]{2,1,0:T(8,128)(2,1)S(1)}, bf16[4,512,256]{2,1,0:T(8,128)(2,1)S(1)}, u32[]{:S(2)}, u32[]{:S(2)}) collective-permute-start(bf16[4,512,256]{2,1,0:T(8,128)(2,1)S(1)} %copy-done.17), channel_id=1, source_target_pairs={{12,8},{13,9},{14,10},{15,11},{28,24},{29,25},{30,26},{31,27}} | collective-permute-start | bytes 3145736 | tf_op jit(solution)/shard_map/ppermute | solution.py:35
  527.8 82.8 %collective-permute-start.31 = (bf16[4,512,256]{2,1,0:T(8,128)(2,1)S(1)}, bf16[4,512,256]{2,1,0:T(8,128)(2,1)S(1)}, u32[]{:S(2)}, u32[]{:S(2)}) collective-permute-start(bf16[4,512,256]{2,1,0:T(8,128)(2,1)S(1)} %get-tuple-element.73), channel_id=1, source_target_pairs={{0,4},{4,8},{1,5},{5,9},{2,6},{6,10},{3,7},{7,11},{16,20},{20,24},... | collective-permute-start | bytes 3145736 | tf_op jit(solution)/shard_map/ppermute | solution.py:34
  547.5 63.8 %collective-permute-start.34 = (bf16[4,512,256]{2,1,0:T(8,128)(2,1)S(1)}, bf16[4,512,256]{2,1,0:T(8,128)(2,1)S(1)}, u32[]{:S(2)}, u32[]{:S(2)}) collective-permute-start(bf16[4,512,256]{2,1,0:T(8,128)(2,1)S(1)} %get-tuple-element.74), channel_id=1, source_target_pairs={{8,4},{12,8},{9,5},{13,9},{10,6},{14,10},{11,7},{15,11},{24,20},{2... | collective-permute-start | bytes 3145736 | tf_op jit(solution)/shard_map/ppermute | solution.py:35
  548.3 55.4 %collective-permute-start.56 = (bf16[2048,128]{0,1:T(8,128)(2,1)S(1)}, bf16[2048,128]{0,1:T(8,128)(2,1)S(1)}, u32[]{:S(2)}, u32[]{:S(2)}) collective-permute-start(bf16[2048,128]{0,1:T(8,128)(2,1)S(1)} %get-tuple-element.67), channel_id=1, source_target_pairs={{0,4},{4,8},{8,12},{1,5},{5,9},{9,13},{2,6},{6,10},{10,14},{3,7},{... | collective-permute-start | bytes 1572872 | tf_op jit(solution)/shard_map/ppermute | solution.py:34
  572.7 53.5 %collective-permute-start.37 = (bf16[4,512,256]{2,1,0:T(8,128)(2,1)S(1)}, bf16[4,512,256]{2,1,0:T(8,128)(2,1)S(1)}, u32[]{:S(2)}, u32[]{:S(2)}) collective-permute-start(bf16[4,512,256]{2,1,0:T(8,128)(2,1)S(1)} %get-tuple-element.75), channel_id=1, source_target_pairs={{0,4},{4,8},{1,5},{5,9},{2,6},{6,10},{3,7},{7,11},{16,20},{20,24},... | collective-permute-start | bytes 3145736 | tf_op jit(solution)/shard_map/ppermute | solution.py:34
  604.5 44.2 %collective-permute-start.43 = (bf16[4,512,256]{2,1,0:T(8,128)(2,1)S(1)}, bf16[4,512,256]{2,1,0:T(8,128)(2,1)S(1)}, u32[]{:S(2)}, u32[]{:S(2)}) collective-permute-start(bf16[4,512,256]{2,1,0:T(8,128)(2,1)S(1)} %get-tuple-element.77), channel_id=1, source_target_pairs={{0,4},{4,8},{1,5},{5,9},{2,6},{6,10},{3,7},{7,11},{16,20},{20,24},... | collective-permute-start | bytes 3145736 | tf_op jit(solution)/shard_map/ppermute | solution.py:34
  610.6 41.8 %collective-permute-start.46 = (bf16[4,512,256]{2,1,0:T(8,128)(2,1)S(1)}, bf16[4,512,256]{2,1,0:T(8,128)(2,1)S(1)}, u32[]{:S(2)}, u32[]{:S(2)}) collective-permute-start(bf16[4,512,256]{2,1,0:T(8,128)(2,1)S(1)} %get-tuple-element.78), channel_id=1, source_target_pairs={{8,4},{12,8},{9,5},{13,9},{10,6},{14,10},{11,7},{15,11},{24,20},{2... | collective-permute-start | bytes 3145736 | tf_op jit(solution)/shard_map/ppermute | solution.py:35
  611.4 59.8 %collective-permute-start.49 = (bf16[4,512,256]{2,1,0:T(8,128)(2,1)S(1)}, bf16[4,512,256]{2,1,0:T(8,128)(2,1)S(1)}, u32[]{:S(2)}, u32[]{:S(2)}) collective-permute-start(bf16[4,512,256]{2,1,0:T(8,128)(2,1)S(1)} %get-tuple-element.79), channel_id=1, source_target_pairs={{0,4},{4,8},{1,5},{5,9},{2,6},{6,10},{3,7},{7,11},{16,20},{20,24},... | collective-permute-start | bytes 3145736 | tf_op jit(solution)/shard_map/ppermute | solution.py:34
  626.2 53.6 %collective-permute-start.52 = (bf16[4,512,256]{2,1,0:T(8,128)(2,1)}, bf16[4,512,256]{2,1,0:T(8,128)(2,1)}, u32[]{:S(2)}, u32[]{:S(2)}) collective-permute-start(bf16[4,512,256]{2,1,0:T(8,128)(2,1)} %get-tuple-element.80), channel_id=1, source_target_pairs={{8,4},{12,8},{9,5},{13,9},{10,6},{14,10},{11,7},{15,11},{24,20},{2... | collective-permute-start | bytes 3145736 | tf_op jit(solution)/shard_map/ppermute | solution.py:35
  629.1 64.6 %collective-permute-start.32 = (bf16[4,512,256]{2,1,0:T(8,128)(2,1)}, bf16[4,512,256]{2,1,0:T(8,128)(2,1)}, u32[]{:S(2)}, u32[]{:S(2)}) collective-permute-start(bf16[4,512,256]{2,1,0:T(8,128)(2,1)} %add.117), channel_id=1, source_target_pairs={{0,4},{4,8},{8,12},{1,5},{5,9},{9,13},{2,6},{6,10},{10,14},{3,7},{... | collective-permute-start | bytes 3145736 | tf_op jit(solution)/shard_map/ppermute | solution.py:34
  648.7 46.3 %collective-permute-start.35 = (bf16[4,512,256]{2,1,0:T(8,128)(2,1)}, bf16[4,512,256]{2,1,0:T(8,128)(2,1)}, u32[]{:S(2)}, u32[]{:S(2)}) collective-permute-start(bf16[4,512,256]{2,1,0:T(8,128)(2,1)} %add.120), channel_id=1, source_target_pairs={{4,0},{8,4},{12,8},{5,1},{9,5},{13,9},{6,2},{10,6},{14,10},{7,3},{... | collective-permute-start | bytes 3145736 | tf_op jit(solution)/shard_map/ppermute | solution.py:35
  652.5 63.7 %collective-permute-start.38 = (bf16[4,512,256]{2,1,0:T(8,128)(2,1)}, bf16[4,512,256]{2,1,0:T(8,128)(2,1)}, u32[]{:S(2)}, u32[]{:S(2)}) collective-permute-start(bf16[4,512,256]{2,1,0:T(8,128)(2,1)} %add.123), channel_id=1, source_target_pairs={{0,4},{4,8},{8,12},{1,5},{5,9},{9,13},{2,6},{6,10},{10,14},{3,7},{... | collective-permute-start | bytes 3145736 | tf_op jit(solution)/shard_map/ppermute | solution.py:34
  671.1 46.6 %collective-permute-start.41 = (bf16[4,512,256]{2,1,0:T(8,128)(2,1)}, bf16[4,512,256]{2,1,0:T(8,128)(2,1)}, u32[]{:S(2)}, u32[]{:S(2)}) collective-permute-start(bf16[4,512,256]{2,1,0:T(8,128)(2,1)} %add.126), channel_id=1, source_target_pairs={{4,0},{8,4},{12,8},{5,1},{9,5},{13,9},{6,2},{10,6},{14,10},{7,3},{... | collective-permute-start | bytes 3145736 | tf_op jit(solution)/shard_map/ppermute | solution.py:35
  679.8 58.9 %collective-permute-start.44 = (bf16[4,512,256]{2,1,0:T(8,128)(2,1)}, bf16[4,512,256]{2,1,0:T(8,128)(2,1)}, u32[]{:S(2)}, u32[]{:S(2)}) collective-permute-start(bf16[4,512,256]{2,1,0:T(8,128)(2,1)} %add.129), channel_id=1, source_target_pairs={{0,4},{4,8},{8,12},{1,5},{5,9},{9,13},{2,6},{6,10},{10,14},{3,7},{... | collective-permute-start | bytes 3145736 | tf_op jit(solution)/shard_map/ppermute | solution.py:34
  693.7 44.9 %collective-permute-start.47 = (bf16[4,512,256]{2,1,0:T(8,128)(2,1)}, bf16[4,512,256]{2,1,0:T(8,128)(2,1)}, u32[]{:S(2)}, u32[]{:S(2)}) collective-permute-start(bf16[4,512,256]{2,1,0:T(8,128)(2,1)} %add.132), channel_id=1, source_target_pairs={{4,0},{8,4},{12,8},{5,1},{9,5},{13,9},{6,2},{10,6},{14,10},{7,3},{... | collective-permute-start | bytes 3145736 | tf_op jit(solution)/shard_map/ppermute | solution.py:35
  695.0 63.8 %collective-permute-start.50 = (bf16[4,512,256]{2,1,0:T(8,128)(2,1)}, bf16[4,512,256]{2,1,0:T(8,128)(2,1)}, u32[]{:S(2)}, u32[]{:S(2)}) collective-permute-start(bf16[4,512,256]{2,1,0:T(8,128)(2,1)} %add.135), channel_id=1, source_target_pairs={{0,4},{4,8},{8,12},{1,5},{5,9},{9,13},{2,6},{6,10},{10,14},{3,7},{... | collective-permute-start | bytes 3145736 | tf_op jit(solution)/shard_map/ppermute | solution.py:34
  716.2 42.7 %collective-permute-start.53 = (bf16[4,512,256]{2,1,0:T(8,128)(2,1)}, bf16[4,512,256]{2,1,0:T(8,128)(2,1)}, u32[]{:S(2)}, u32[]{:S(2)}) collective-permute-start(bf16[4,512,256]{2,1,0:T(8,128)(2,1)} %add.138), channel_id=1, source_target_pairs={{4,0},{8,4},{12,8},{5,1},{9,5},{13,9},{6,2},{10,6},{14,10},{7,3},{... | collective-permute-start | bytes 3145736 | tf_op jit(solution)/shard_map/ppermute | solution.py:35
  (66 other events, 1818.6 us)
Sparse Core Ops, SparseCore 0:
  10.2 49.0 all-gather.1
  417.7 32.5 all-reduce.2
  453.0 58.3 reduce-scatter.1

commit v2 on v1

--- a/solution.py
+++ b/solution.py
@@ -12,6 +12,13 @@
 CHUNKS = 4
 F32 = jnp.float32
 BF16 = jnp.bfloat16
+
+
+def after(index, *arrays):
+    for a in arrays:
+        corner = a[(0,) * a.ndim]
+        index = index + (corner != corner).astype(jnp.int32)
+    return index
 
 
 def line_gather(own, n):
@@ -21,11 +28,13 @@
         left_pairs = [(d, d - 1) for d in range(1, n) if d + (m - 1) <= n - 1]
         from_left[m] = lax.ppermute(own if m == 1 else from_left[m - 1], "dp", right_pairs)
         from_right[m] = lax.ppermute(own if m == 1 else from_right[m - 1], "dp", left_pairs)
-    return [(from_left[m], from_right[n - m]) for m in range(1, n)]
+    late = max(1, n - 2)
+    return [(from_left[m], from_right[n - m]) for m in range(1, n)], (from_left[late], from_right[late])
 
 
 def line_scatter(terms, n):
     got_left = got_right = None
+    steps = []
     for m in range(n - 1, 0, -1):
         right_pairs = [(d, d + 1) for d in range(n - 1) if d + m <= n - 1]
         left_pairs = [(d, d - 1) for d in range(1, n) if d - m >= 0]
@@ -33,7 +42,8 @@
         to_left = terms[n - m] if got_right is None else terms[n - m] + got_right
         got_left = lax.ppermute(to_right, "dp", right_pairs)
         got_right = lax.ppermute(to_left, "dp", left_pairs)
-    return terms[0].astype(F32) + got_left.astype(F32) + got_right.astype(F32)
+        steps.append((got_left, got_right))
+    return terms[0].astype(F32) + got_left.astype(F32) + got_right.astype(F32), steps
 
 
 def chunk_kernel(n, slots, bs, first, base, where_ref, pattern_ref, x_ref, xt_ref, ra_ref, rat_ref, cot_ref, *rest):
@@ -149,11 +159,16 @@
     me = lax.axis_index("dp").astype(jnp.int32).reshape(1)
     local_pattern = lax.dynamic_slice_in_dim(pattern, lax.axis_index("tensor") * local_cols, local_cols, 0)
 
-    left_pairs = line_gather(left_factor, n)
+    left_pairs, _ = line_gather(left_factor, n)
     packed = jnp.concatenate(
         [blocks.reshape(local_cols, slots * cs, bs), right_factor.reshape(rs, local_cols, bs).transpose(1, 0, 2)], axis=1
     )
-    gathered = [line_gather(packed[c * cj : (c + 1) * cj], n) for c in range(CHUNKS)]
+    gathered = []
+    waits = ()
+    for c in range(CHUNKS):
+        part = lax.dynamic_slice_in_dim(packed, after(jnp.int32(c * cj), *waits), cj, 0)
+        pairs, waits = line_gather(part, n)
+        gathered.append(pairs)
 
     x = lax.all_gather(tokens, "tensor", axis=1, tiled=True)
     xt = x.T
@@ -163,19 +178,27 @@
 
     carried = None
     sums = []
+    steps = []
     for c in range(CHUNKS):
+        where = me
+        if c >= 1:
+            where = after(where, *steps[c - 1][0])
+        if c >= 2:
+            where = after(where, *steps[c - 2][-1])
         hidden, acc, terms = run_chunk(
-            n, slots, bs, c * cj, cj, me, local_pattern, x, xt, rank_acts, rank_acts_t, cotangent, packed, gathered[c], carried
+            n, slots, bs, c * cj, cj, where, local_pattern, x, xt, rank_acts, rank_acts_t, cotangent, packed, gathered[c], carried
         )
         carried = (acc, hidden)
-        sums.append(line_scatter(list(terms), n))
+        total, got = line_scatter(list(terms), n)
+        sums.append(total)
+        steps.append(got)
 
     width = x.shape[1]
     rank_grad = lax.psum(acc[:, width:].astype(BF16), "tensor")
     token_part = lax.psum_scatter(acc[:, :width].astype(BF16), "tensor", scatter_dimension=1, tiled=True).astype(F32)
     left_term = lax.dot_general(tokens, rank_grad, (((0,), (0,)), ((), ())), preferred_element_type=F32).astype(BF16)
     left_terms = [left_term[:, ((n - r) % n) * rw : ((n - r) % n + 1) * rw] for r in range(n)]
-    left_grad = line_scatter(left_terms, n)
+    left_grad, _ = line_scatter(left_terms, n)
     token_grad = token_part + lax.dot_general(
         rank_grad, left_rot, (((1,), (1,)), ((), ())), preferred_element_type=F32
     )

time: 788 us -> 720 us (0.914)
  waiting for transfers between devices: 388 us -> 269 us
  between operations: 14.9 us -> 35.4 us
  other arithmetic: 45.1 us -> 62 us
  local copies, waits for them, and re-layouts: 39.8 us -> 54 us
    ppermute x15, waiting for transfers between devices: 141 us -> 85.7 us  [line_gather(): lax.ppermute(own if m == 1 else from_right[m - 1], 'dp', left_pairs)]
    ppermute x15, waiting for transfers between devices: 172 us -> 123 us  [line_scatter(): got_left = lax.ppermute(to_right, 'dp', right_pairs)]
    slice x0 -> x16, local copies, waits for them, and re-layouts: none -> 14.2 us  [after(): corner = a[(0,) * a.ndim]]
    ppermute x15, waiting for transfers between devices: 48.2 us -> 36.7 us  [line_gather(): lax.ppermute(own if m == 1 else from_left[m - 1], 'dp', right_pairs)]
    ppermute x15, starting transfers between devices: 89.2 us -> 81 us  [line_scatter(): got_left = lax.ppermute(to_right, 'dp', right_pairs)]
    unnamed x103 -> x95, local copies, waits for them, and re-layouts: 16.3 us -> 14.9 us
  transfers between devices with their start and end apart: 63 -> 63, of which waited for: 25 -> 20; matrix products, arithmetic and copies ran while one was open for 9% -> 14% of each run, Pallas kernels for 10% -> 11%
where the time goes in v2:
time: 720 us; the launch traced here: 717 us
  waiting for transfers between devices  269 us (37%)
  starting transfers between devices  163 us (23%)
  Pallas kernels  104 us (14%)
  other arithmetic  62 us (9%)
  local copies, waits for them, and re-layouts  54 us (8%)
  between operations  35.4 us (5%)
  blocking collectives  20.4 us (3%)
  matrix products  9.31 us (1%)
    ppermute x15, waiting for transfers between devices, line_scatter(): got_left = lax.ppermute(to_right, 'dp', right_pairs)  123 us
    pallas_call x4, Pallas kernels, run_chunk(): pl.pallas_call(functools.partial(chunk_kernel, n, slots, bs, first, base)...  104 us
    ppermute x15, waiting for transfers between devices, line_gather(): lax.ppermute(own if m == 1 else from_right[m - 1], 'dp', left_pairs)  85.7 us
    ppermute x15, starting transfers between devices, line_scatter(): got_left = lax.ppermute(to_right, 'dp', right_pairs)  81 us
    ppermute x15, starting transfers between devices, line_gather(): lax.ppermute(own if m == 1 else from_left[m - 1], 'dp', right_pairs)  43.6 us
    ppermute x15, waiting for transfers between devices, line_gather(): lax.ppermute(own if m == 1 else from_left[m - 1], 'dp', right_pairs)  36.7 us
    psum x1, blocking collectives, per_device(): lax.psum(jnp.dot(tokens, left_rot, preferred_element_type=F32), 'tensor')  20.4 us
    psum x1, waiting for transfers between devices, per_device(): rank_grad = lax.psum(acc[:, width:].astype(BF16), 'tensor')  19.4 us
  transfers between devices with their start and end apart: 63, of which 20 were waited for; matrix products, arithmetic and copies ran while one was open for 14% of the time, Pallas kernels for 11%

profile of v2, /device:TPU:0, one launch (start us, length us, event | category | flops | bytes accessed | tf_op | source)
XLA Modules:
  0.0 717.2 jit_solution(17183665308422648855)
XLA Ops:
  15.6 5.0 collective-permute-start.6
  21.9 21.0 %collective-permute-done.6.rest_1_ = bf16[4,512,256]{2,1,0:T(8,128)(2,1)S(1)} collective-permute-done((bf16[4,512,256]{2,1,0:T(8,128)(2,1)S(1)}, bf16[4,512,256]{2,1,0:T(8,128)(2,1)S(1)}, u32[]{:S(2)}, u32[]{:S(2)}) %collective-permute-start.6) | collective-permute-done | bytes 1048608 | tf_op jit(solution)/shard_map/ppermute | solution.py:29
  50.9 24.1 %collective-permute-done.8.rest_4_ = bf16[4,512,256]{2,1,0:T(8,128)(2,1)} collective-permute-done((bf16[4,512,256]{2,1,0:T(8,128)(2,1)S(1)}, bf16[4,512,256]{2,1,0:T(8,128)(2,1)}, u32[]{:S(2)}, u32[]{:S(2)}) %collective-permute-start.8) | collective-permute-done | bytes 1048608 | tf_op jit(solution)/shard_map/ppermute | solution.py:30
  78.5 4.6 collective-permute-start.14
  85.8 5.2 collective-permute-start
  91.0 28.0 %collective-permute-done.1 = bf16[2048,128]{1,0:T(8,128)(2,1)S(1)} collective-permute-done((bf16[2048,128]{1,0:T(8,128)(2,1)S(1)}, bf16[2048,128]{1,0:T(8,128)(2,1)S(1)}, u32[]{:S(2)}, u32[]{:S(2)}) %collective-permute-start.1) | collective-permute-done | bytes 524320 | tf_op jit(solution)/shard_map/ppermute | solution.py:30
  124.7 10.6 %collective-permute-done.2 = bf16[2048,128]{1,0:T(8,128)(2,1)} collective-permute-done((bf16[2048,128]{1,0:T(8,128)(2,1)S(1)}, bf16[2048,128]{1,0:T(8,128)(2,1)}, u32[]{:S(2)}, u32[]{:S(2)}) %collective-permute-start.2) | collective-permute-done | bytes 524320 | tf_op jit(solution)/shard_map/ppermute | solution.py:30
  138.9 3.6 pad_maximum_fusion.rest_0_
  144.0 21.2 %collective-permute-done.3 = bf16[2048,128]{1,0:T(8,128)(2,1)} collective-permute-done((bf16[2048,128]{1,0:T(8,128)(2,1)}, bf16[2048,128]{1,0:T(8,128)(2,1)}, u32[]{:S(2)}, u32[]{:S(2)}) %collective-permute-start.3) | collective-permute-done | bytes 524320 | tf_op jit(solution)/shard_map/ppermute | solution.py:30
  181.1 20.4 %all-reduce.4 = bf16[384,512]{0,1:T(8,128)(2,1)S(1)} all-reduce(f32[384,512]{0,1:T(8,128)} %convolution_bitcast_fusion), channel_id=1, replica_groups=mesh['pipe'=2,'dp'=4,'tensor'=4] {'tensor'}, use_global_device_ids=true, to_apply=%region_0.0 | all-reduce | flops 196608 | bytes 1179648 | tf_op jit(solution)/shard_map/psum | solution.py:176
  202.5 7.1 collective-permute-start.26
  209.6 8.6 %copy.32.x_ref = bf16[384,8192]{1,0:T(8,128)(2,1)} copy(bf16[384,8192]{0,1:T(8,128)(2,1)} %all-gather.2.cloned.1.call-done) | data formatting | bytes 12582912 | tf_op jit(solution)/shard_map/all_gather | solution.py:173
  218.2 22.9 %shard_map.101 = (bf16[384,4096]{1,0:T(8,128)(2,1)}, f32[384,8704]{1,0:T(8,128)}, bf16[4,512,256]{2,1,0:T(8,128)(2,1)}, bf16[4,512,256]{2,1,0:T(8,128)(2,1)}, bf...) custom-call(s32[1]{0:T(128)} %bitcast.where_ref, s32[16,6]{1,0:T(8,128)} %copy.46.pattern_ref, ...), custom_call_target="tpu_custom_call" | custom-call | flops 4831838208 | bytes 50000000 | tf_op jit(solution)/shard_map/pallas_call | solution.py:131
  241.2 3.1 collective-permute-start.12
  249.2 17.4 %collective-permute-done.12 = bf16[4,512,256]{2,1,0:T(8,128)(2,1)S(1)} collective-permute-done((bf16[4,512,256]{2,1,0:T(8,128)(2,1)}, bf16[4,512,256]{2,1,0:T(8,128)(2,1)S(1)}, u32[]{:S(2)}, u32[]{:S(2)}) %collective-permute-start.12) | collective-permute-done | bytes 1048608 | tf_op jit(solution)/shard_map/ppermute | solution.py:43
  276.2 27.0 %shard_map.102 = (bf16[384,4096]{1,0:T(8,128)(2,1)}, f32[384,8704]{1,0:T(8,128)}, bf16[4,512,256]{2,1,0:T(8,128)(2,1)}, bf16[4,512,256]{2,1,0:T(8,128)(2,1)}, bf...) custom-call(s32[1]{0:T(128)S(6)} %add.237.where_ref, ...), custom_call_target="tpu_custom_call", output_to_operand_aliasing={{1}: (14, {}), {0}: (15, {})} | custom-call | flops 4831838208 | bytes 50000000 | tf_op jit(solution)/shard_map/pallas_call | solution.py:131
  303.3 5.8 collective-permute-start.20
  319.6 5.5 collective-permute-start.38
  326.5 5.5 collective-permute-done.20
  336.0 18.5 %collective-permute-done.22 = bf16[4,512,256]{2,1,0:T(8,128)(2,1)S(1)} collective-permute-done((bf16[4,512,256]{2,1,0:T(8,128)(2,1)}, bf16[4,512,256]{2,1,0:T(8,128)(2,1)S(1)}, u32[]{:S(2)}, u32[]{:S(2)}) %collective-permute-start.22) | collective-permute-done | bytes 1048608 | tf_op jit(solution)/shard_map/ppermute | solution.py:43
  354.8 4.5 collective-permute-start.23
  361.2 15.6 %collective-permute-done.38.rest_1_ = bf16[4,512,256]{2,1,0:T(8,128)(2,1)} collective-permute-done((bf16[4,512,256]{2,1,0:T(8,128)(2,1)S(1)}, bf16[4,512,256]{2,1,0:T(8,128)(2,1)}, u32[]{:S(2)}, u32[]{:S(2)}) %collective-permute-start.38) | collective-permute-done | bytes 1048608 | tf_op jit(solution)/shard_map/ppermute | solution.py:29
  382.4 16.9 %collective-permute-done.23 = bf16[4,512,256]{2,1,0:T(8,128)(2,1)S(1)} collective-permute-done((bf16[4,512,256]{2,1,0:T(8,128)(2,1)S(1)}, bf16[4,512,256]{2,1,0:T(8,128)(2,1)S(1)}, u32[]{:S(2)}, u32[]{:S(2)}) %collective-permute-start.23) | collective-permute-done | bytes 1048608 | tf_op jit(solution)/shard_map/ppermute | solution.py:43
  400.9 18.5 %collective-permute-done.34 = bf16[4,512,256]{2,1,0:T(8,128)(2,1)S(1)} collective-permute-done((bf16[4,512,256]{2,1,0:T(8,128)(2,1)S(1)}, bf16[4,512,256]{2,1,0:T(8,128)(2,1)S(1)}, u32[]{:S(2)}, u32[]{:S(2)}) %collective-permute-start.34) | collective-permute-done | bytes 1048608 | tf_op jit(solution)/shard_map/ppermute | solution.py:43
  430.5 6.0 collective-permute-start.35
  436.5 27.0 %shard_map.103 = (bf16[384,4096]{1,0:T(8,128)(2,1)}, f32[384,8704]{1,0:T(8,128)}, bf16[4,512,256]{2,1,0:T(8,128)(2,1)}, bf16[4,512,256]{2,1,0:T(8,128)(2,1)}, bf...) custom-call(s32[1]{0:T(128)S(6)} %add.256.where_ref, ...), custom_call_target="tpu_custom_call", output_to_operand_aliasing={{1}: (14, {}), {0}: (15, {})} | custom-call | flops 4831838208 | bytes 50000000 | tf_op jit(solution)/shard_map/pallas_call | solution.py:131
  463.6 3.1 collective-permute-start.32
  474.7 12.1 %collective-permute-done.32 = bf16[4,512,256]{2,1,0:T(8,128)(2,1)S(1)} collective-permute-done((bf16[4,512,256]{2,1,0:T(8,128)(2,1)}, bf16[4,512,256]{2,1,0:T(8,128)(2,1)S(1)}, u32[]{:S(2)}, u32[]{:S(2)}) %collective-permute-start.32) | collective-permute-done | bytes 1048608 | tf_op jit(solution)/shard_map/ppermute | solution.py:43
  491.8 27.1 %shard_map.104 = (bf16[384,4096]{1,0:T(8,128)(2,1)}, f32[384,8704]{1,0:T(8,128)}, bf16[4,512,256]{2,1,0:T(8,128)(2,1)}, bf16[4,512,256]{2,1,0:T(8,128)(2,1)}, bf...) custom-call(s32[1]{0:T(128)S(6)} %add.275.where_ref, ...), custom_call_target="tpu_custom_call", output_to_operand_aliasing={{1}: (14, {}), {0}: (15, {})} | custom-call | flops 4831838208 | bytes 50000000 | tf_op jit(solution)/shard_map/pallas_call | solution.py:131
  518.9 8.2 %convert.14 = bf16[384,8704]{1,0:T(8,128)(2,1)} convert(f32[384,8704]{1,0:T(8,128)} %get-tuple-element.44) | non-fusion elementwise | flops 3342336 | bytes 20054016 | tf_op jit(solution)/shard_map/convert.11
  528.9 6.1 slice.138
  535.0 5.2 collective-permute-start.48
  541.9 19.4 %all-reduce.3.cloned.1.call-done = bf16[384,512]{1,0:T(8,128)(2,1)} async-done(((bf16[384,512]{1,0:T(8,128)(2,1)}), bf16[384,512]{1,0:T(8,128)(2,1)}) %all-reduce.3.cloned.1.call-update) | async-done | bytes 393232 | tf_op jit(solution)/shard_map/psum | solution.py:197
  563.8 3.6 collective-permute-start.54
  572.1 7.7 %collective-permute-done.54 = bf16[2048,128]{0,1:T(8,128)(2,1)S(1)} collective-permute-done((bf16[2048,128]{0,1:T(8,128)(2,1)S(1)}, bf16[2048,128]{0,1:T(8,128)(2,1)S(1)}, u32[]{:S(2)}, u32[]{:S(2)}) %collective-permute-start.54) | collective-permute-done | bytes 524320 | tf_op jit(solution)/shard_map/ppermute | solution.py:43
  582.5 4.8 collective-permute-start.55
  588.8 3.2 fusion.9
  592.1 4.6 collective-permute-start.49
  599.4 2.9 collective-permute-done.44
  605.1 5.5 collective-permute-start.45
  618.6 5.5 collective-permute-start.56
  624.1 12.0 %collective-permute-done.49 = bf16[4,512,256]{2,1,0:T(8,128)(2,1)} collective-permute-done((bf16[4,512,256]{2,1,0:T(8,128)(2,1)}, bf16[4,512,256]{2,1,0:T(8,128)(2,1)}, u32[]{:S(2)}, u32[]{:S(2)}) %collective-permute-start.49) | collective-permute-done | bytes 1048608 | tf_op jit(solution)/shard_map/ppermute | solution.py:43
  644.2 23.5 %collective-permute-start.50 = (bf16[4,512,256]{2,1,0:T(8,128)(2,1)}, bf16[4,512,256]{2,1,0:T(8,128)(2,1)}, u32[]{:S(2)}, u32[]{:S(2)}) collective-permute-start(bf16[4,512,256]{2,1,0:T(8,128)(2,1)} %add.291), channel_id=1, source_target_pairs={{0,4},{4,8},{8,12},{1,5},{5,9},{9,13},{2,6},{6,10},{10,14},{3,7},{... | collective-permute-start | bytes 3145736 | tf_op jit(solution)/shard_map/ppermute | solution.py:43
  678.0 11.9 %collective-permute-done.50 = bf16[4,512,256]{2,1,0:T(8,128)(2,1)} collective-permute-done((bf16[4,512,256]{2,1,0:T(8,128)(2,1)}, bf16[4,512,256]{2,1,0:T(8,128)(2,1)}, u32[]{:S(2)}, u32[]{:S(2)}) %collective-permute-start.50) | collective-permute-done | bytes 1048608 | tf_op jit(solution)/shard_map/ppermute | solution.py:43
  689.9 3.3 collective-permute-done.53
  698.3 3.0 copy.45
  701.3 4.5 pad_maximum_fusion.1
  705.9 4.8 convert_add_fusion
  (251 shorter events, 146.0 us)
Async XLA Ops:
  7.2 202.4 %all-gather.2.cloned.1.call-start = ((), (), s32[]{:S(2)}) async-start(), calls=%async_computation.1 | async-start | bytes 7864320 | tf_op jit(solution)/shard_map/all_gather | solution.py:173
  9.8 551.5 %all-reduce.3.cloned.1.call-start = ((), (), s32[]{:S(2)}) async-start(), calls=%async_computation.3 | async-start | bytes 786432 | tf_op jit(solution)/shard_map/psum | solution.py:197
  47.1 27.8 %collective-permute-start.8 = (bf16[4,512,256]{2,1,0:T(8,128)(2,1)S(1)}, bf16[4,512,256]{2,1,0:T(8,128)(2,1)}, u32[]{:S(2)}, u32[]{:S(2)}) collective-permute-start(bf16[4,512,256]{2,1,0:T(8,128)(2,1)S(1)} %collective-permute-done.7.rest_6_), channel_id=1, source_target_pairs={{4,0},{8,4},{5,1},{9,5},{6,2},{10,6},{7,3},{11,7},{20,16},{24,20},... | collective-permute-start | bytes 3145736 | tf_op jit(solution)/shard_map/ppermute | solution.py:30
  78.5 43.2 %collective-permute-start.14 = (bf16[4,512,256]{2,1,0:T(8,128)(2,1)S(1)}, bf16[4,512,256]{2,1,0:T(8,128)(2,1)}, u32[]{:S(2)}, u32[]{:S(2)}) collective-permute-start(bf16[4,512,256]{2,1,0:T(8,128)(2,1)S(1)} %fusion.2), channel_id=1, source_target_pairs={{0,4},{4,8},{8,12},{1,5},{5,9},{9,13},{2,6},{6,10},{10,14},{3,7},{... | collective-permute-start | bytes 3145736 | tf_op jit(solution)/shard_map/ppermute | solution.py:29
  83.2 40.2 %collective-permute-start.15 = (bf16[4,512,256]{2,1,0:T(8,128)(2,1)S(1)}, bf16[4,512,256]{2,1,0:T(8,128)(2,1)}, u32[]{:S(2)}, u32[]{:S(2)}) collective-permute-start(bf16[4,512,256]{2,1,0:T(8,128)(2,1)S(1)} %fusion.2), channel_id=1, source_target_pairs={{4,0},{8,4},{12,8},{5,1},{9,5},{13,9},{6,2},{10,6},{14,10},{7,3},{... | collective-permute-start | bytes 3145736 | tf_op jit(solution)/shard_map/ppermute | solution.py:30
  84.5 34.5 %collective-permute-start.1 = (bf16[2048,128]{1,0:T(8,128)(2,1)S(1)}, bf16[2048,128]{1,0:T(8,128)(2,1)S(1)}, u32[]{:S(2)}, u32[]{:S(2)}) collective-permute-start(bf16[2048,128]{1,0:T(8,128)(2,1)S(1)} %copy-done.42), channel_id=1, source_target_pairs={{4,0},{8,4},{12,8},{5,1},{9,5},{13,9},{6,2},{10,6},{14,10},{7,3},{... | collective-permute-start | bytes 1572872 | tf_op jit(solution)/shard_map/ppermute | solution.py:30
  85.8 34.5 %collective-permute-start = (bf16[2048,128]{1,0:T(8,128)(2,1)S(1)}, bf16[2048,128]{1,0:T(8,128)(2,1)S(1)}, u32[]{:S(2)}, u32[]{:S(2)}) collective-permute-start(bf16[2048,128]{1,0:T(8,128)(2,1)S(1)} %copy-done.42), channel_id=1, source_target_pairs={{0,4},{4,8},{8,12},{1,5},{5,9},{9,13},{2,6},{6,10},{10,14},{3,7},{... | collective-permute-start | bytes 1572872 | tf_op jit(solution)/shard_map/ppermute | solution.py:29
  121.8 51.1 %collective-permute-start.18 = (bf16[4,512,256]{2,1,0:T(8,128)(2,1)}, bf16[4,512,256]{2,1,0:T(8,128)(2,1)}, u32[]{:S(2)}, u32[]{:S(2)}) collective-permute-start(bf16[4,512,256]{2,1,0:T(8,128)(2,1)} %collective-permute-done.14.rest_1_), channel_id=1, source_target_pairs={{4,8},{8,12},{5,9},{9,13},{6,10},{10,14},{7,11},{11,15},{20,24},{2... | collective-permute-start | bytes 3145736 | tf_op jit(solution)/shard_map/ppermute | solution.py:29
  123.4 51.9 %collective-permute-start.16 = (bf16[4,512,256]{2,1,0:T(8,128)(2,1)}, bf16[4,512,256]{2,1,0:T(8,128)(2,1)}, u32[]{:S(2)}, u32[]{:S(2)}) collective-permute-start(bf16[4,512,256]{2,1,0:T(8,128)(2,1)} %collective-permute-done.15.rest_6_), channel_id=1, source_target_pairs={{4,0},{8,4},{5,1},{9,5},{6,2},{10,6},{7,3},{11,7},{20,16},{24,20},... | collective-permute-start | bytes 3145736 | tf_op jit(solution)/shard_map/ppermute | solution.py:30
  135.3 29.8 %collective-permute-start.3 = (bf16[2048,128]{1,0:T(8,128)(2,1)}, bf16[2048,128]{1,0:T(8,128)(2,1)}, u32[]{:S(2)}, u32[]{:S(2)}) collective-permute-start(bf16[2048,128]{1,0:T(8,128)(2,1)} %collective-permute-done.2), channel_id=1, source_target_pairs={{4,0},{5,1},{6,2},{7,3},{20,16},{21,17},{22,18},{23,19}} | collective-permute-start | bytes 1572872 | tf_op jit(solution)/shard_map/ppermute | solution.py:30
  136.6 29.7 %collective-permute-start.5 = (bf16[2048,128]{1,0:T(8,128)(2,1)}, bf16[2048,128]{1,0:T(8,128)(2,1)}, u32[]{:S(2)}, u32[]{:S(2)}) collective-permute-start(bf16[2048,128]{1,0:T(8,128)(2,1)} %collective-permute-done.4), channel_id=1, source_target_pairs={{8,12},{9,13},{10,14},{11,15},{24,28},{25,29},{26,30},{27,31}} | collective-permute-start | bytes 1572872 | tf_op jit(solution)/shard_map/ppermute | solution.py:29
  167.8 50.4 %collective-permute-start.11 = (bf16[4,512,256]{2,1,0:T(8,128)(2,1)}, bf16[4,512,256]{2,1,0:T(8,128)(2,1)}, u32[]{:S(2)}, u32[]{:S(2)}) collective-permute-start(bf16[4,512,256]{2,1,0:T(8,128)(2,1)} %collective-permute-done.10.rest_3_), channel_id=1, source_target_pairs={{8,12},{9,13},{10,14},{11,15},{24,28},{25,29},{26,30},{27,31}} | collective-permute-start | bytes 3145736 | tf_op jit(solution)/shard_map/ppermute | solution.py:29
  169.4 48.8 %collective-permute-start.9 = (bf16[4,512,256]{2,1,0:T(8,128)(2,1)}, bf16[4,512,256]{2,1,0:T(8,128)(2,1)}, u32[]{:S(2)}, u32[]{:S(2)}) collective-permute-start(bf16[4,512,256]{2,1,0:T(8,128)(2,1)} %collective-permute-done.8.rest_4_), channel_id=1, source_target_pairs={{4,0},{5,1},{6,2},{7,3},{20,16},{21,17},{22,18},{23,19}} | collective-permute-start | bytes 3145736 | tf_op jit(solution)/shard_map/ppermute | solution.py:30
  179.8 66.5 %collective-permute-start.27 = (bf16[4,512,256]{2,1,0:T(8,128)(2,1)}, bf16[4,512,256]{2,1,0:T(8,128)(2,1)}, u32[]{:S(2)}, u32[]{:S(2)}) collective-permute-start(bf16[4,512,256]{2,1,0:T(8,128)(2,1)} %fusion.3), channel_id=1, source_target_pairs={{4,0},{8,4},{12,8},{5,1},{9,5},{13,9},{6,2},{10,6},{14,10},{7,3},{... | collective-permute-start | bytes 3145736 | tf_op jit(solution)/shard_map/ppermute | solution.py:30
  202.5 45.5 %collective-permute-start.26 = (bf16[4,512,256]{2,1,0:T(8,128)(2,1)}, bf16[4,512,256]{2,1,0:T(8,128)(2,1)}, u32[]{:S(2)}, u32[]{:S(2)}) collective-permute-start(bf16[4,512,256]{2,1,0:T(8,128)(2,1)} %fusion.3), channel_id=1, source_target_pairs={{0,4},{4,8},{8,12},{1,5},{5,9},{9,13},{2,6},{6,10},{10,14},{3,7},{... | collective-permute-start | bytes 3145736 | tf_op jit(solution)/shard_map/ppermute | solution.py:29
  245.0 31.2 %collective-permute-start.17 = (bf16[4,512,256]{2,1,0:T(8,128)(2,1)}, bf16[4,512,256]{2,1,0:T(8,128)(2,1)}, u32[]{:S(2)}, u32[]{:S(2)}) collective-permute-start(bf16[4,512,256]{2,1,0:T(8,128)(2,1)} %collective-permute-done.16.rest_4_), channel_id=1, source_target_pairs={{4,0},{5,1},{6,2},{7,3},{20,16},{21,17},{22,18},{23,19}} | collective-permute-start | bytes 3145736 | tf_op jit(solution)/shard_map/ppermute | solution.py:30
  246.3 29.9 %collective-permute-start.19 = (bf16[4,512,256]{2,1,0:T(8,128)(2,1)}, bf16[4,512,256]{2,1,0:T(8,128)(2,1)}, u32[]{:S(2)}, u32[]{:S(2)}) collective-permute-start(bf16[4,512,256]{2,1,0:T(8,128)(2,1)} %collective-permute-done.18.rest_3_), channel_id=1, source_target_pairs={{8,12},{9,13},{10,14},{11,15},{24,28},{25,29},{26,30},{27,31}} | collective-permute-start | bytes 3145736 | tf_op jit(solution)/shard_map/ppermute | solution.py:29
  248.0 65.1 %collective-permute-start.28 = (bf16[4,512,256]{2,1,0:T(8,128)(2,1)}, bf16[4,512,256]{2,1,0:T(8,128)(2,1)}, u32[]{:S(2)}, u32[]{:S(2)}) collective-permute-start(bf16[4,512,256]{2,1,0:T(8,128)(2,1)} %collective-permute-done.27.rest_6_), channel_id=1, source_target_pairs={{4,0},{8,4},{5,1},{9,5},{6,2},{10,6},{7,3},{11,7},{20,16},{24,20},... | collective-permute-start | bytes 3145736 | tf_op jit(solution)/shard_map/ppermute | solution.py:30
  266.6 44.1 %collective-permute-start.30 = (bf16[4,512,256]{2,1,0:T(8,128)(2,1)}, bf16[4,512,256]{2,1,0:T(8,128)(2,1)}, u32[]{:S(2)}, u32[]{:S(2)}) collective-permute-start(bf16[4,512,256]{2,1,0:T(8,128)(2,1)} %collective-permute-done.26.rest_1_), channel_id=1, source_target_pairs={{4,8},{8,12},{5,9},{9,13},{6,10},{10,14},{7,11},{11,15},{20,24},{2... | collective-permute-start | bytes 3145736 | tf_op jit(solution)/shard_map/ppermute | solution.py:29
  270.9 48.6 %collective-permute-start.24 = (bf16[4,512,256]{2,1,0:T(8,128)(2,1)}, bf16[4,512,256]{2,1,0:T(8,128)(2,1)}, u32[]{:S(2)}, u32[]{:S(2)}) collective-permute-start(bf16[4,512,256]{2,1,0:T(8,128)(2,1)} %get-tuple-element.75), channel_id=1, source_target_pairs={{8,4},{12,8},{9,5},{13,9},{10,6},{14,10},{11,7},{15,11},{24,20},{2... | collective-permute-start | bytes 3145736 | tf_op jit(solution)/shard_map/ppermute | solution.py:44
  303.3 28.7 %collective-permute-start.20 = (bf16[4,512,256]{2,1,0:T(8,128)(2,1)}, bf16[4,512,256]{2,1,0:T(8,128)(2,1)}, u32[]{:S(2)}, u32[]{:S(2)}) collective-permute-start(bf16[4,512,256]{2,1,0:T(8,128)(2,1)} %get-tuple-element.33), channel_id=1, source_target_pairs={{0,4},{1,5},{2,6},{3,7},{16,20},{17,21},{18,22},{19,23}} | collective-permute-start | bytes 3145736 | tf_op jit(solution)/shard_map/ppermute | solution.py:43
  315.6 38.9 %collective-permute-start.22 = (bf16[4,512,256]{2,1,0:T(8,128)(2,1)}, bf16[4,512,256]{2,1,0:T(8,128)(2,1)S(1)}, u32[]{:S(2)}, u32[]{:S(2)}) collective-permute-start(bf16[4,512,256]{2,1,0:T(8,128)(2,1)} %get-tuple-element.76), channel_id=1, source_target_pairs={{0,4},{4,8},{1,5},{5,9},{2,6},{6,10},{3,7},{7,11},{16,20},{20,24},... | collective-permute-start | bytes 3145736 | tf_op jit(solution)/shard_map/ppermute | solution.py:43
  318.1 41.1 %collective-permute-start.39 = (bf16[4,512,256]{2,1,0:T(8,128)(2,1)S(1)}, bf16[4,512,256]{2,1,0:T(8,128)(2,1)}, u32[]{:S(2)}, u32[]{:S(2)}) collective-permute-start(bf16[4,512,256]{2,1,0:T(8,128)(2,1)S(1)} %fusion.4), channel_id=1, source_target_pairs={{4,0},{8,4},{12,8},{5,1},{9,5},{13,9},{6,2},{10,6},{14,10},{7,3},{... | collective-permute-start | bytes 3145736 | tf_op jit(solution)/shard_map/ppermute | solution.py:30
  319.6 57.3 %collective-permute-start.38 = (bf16[4,512,256]{2,1,0:T(8,128)(2,1)S(1)}, bf16[4,512,256]{2,1,0:T(8,128)(2,1)}, u32[]{:S(2)}, u32[]{:S(2)}) collective-permute-start(bf16[4,512,256]{2,1,0:T(8,128)(2,1)S(1)} %fusion.4), channel_id=1, source_target_pairs={{0,4},{4,8},{8,12},{1,5},{5,9},{9,13},{2,6},{6,10},{10,14},{3,7},{... | collective-permute-start | bytes 3145736 | tf_op jit(solution)/shard_map/ppermute | solution.py:29
  332.0 46.1 %collective-permute-start.25 = (bf16[4,512,256]{2,1,0:T(8,128)(2,1)S(1)}, bf16[4,512,256]{2,1,0:T(8,128)(2,1)S(1)}, u32[]{:S(2)}, u32[]{:S(2)}) collective-permute-start(bf16[4,512,256]{2,1,0:T(8,128)(2,1)S(1)} %add.253), channel_id=1, source_target_pairs={{4,0},{8,4},{12,8},{5,1},{9,5},{13,9},{6,2},{10,6},{14,10},{7,3},{... | collective-permute-start | bytes 3145736 | tf_op jit(solution)/shard_map/ppermute | solution.py:44
  335.1 44.7 %collective-permute-start.36 = (bf16[4,512,256]{2,1,0:T(8,128)(2,1)S(1)}, bf16[4,512,256]{2,1,0:T(8,128)(2,1)S(1)}, u32[]{:S(2)}, u32[]{:S(2)}) collective-permute-start(bf16[4,512,256]{2,1,0:T(8,128)(2,1)S(1)} %get-tuple-element.73), channel_id=1, source_target_pairs={{8,4},{12,8},{9,5},{13,9},{10,6},{14,10},{11,7},{15,11},{24,20},{2... | collective-permute-start | bytes 3145736 | tf_op jit(solution)/shard_map/ppermute | solution.py:44
  354.8 44.5 %collective-permute-start.23 = (bf16[4,512,256]{2,1,0:T(8,128)(2,1)S(1)}, bf16[4,512,256]{2,1,0:T(8,128)(2,1)S(1)}, u32[]{:S(2)}, u32[]{:S(2)}) collective-permute-start(bf16[4,512,256]{2,1,0:T(8,128)(2,1)S(1)} %add.248), channel_id=1, source_target_pairs={{0,4},{4,8},{8,12},{1,5},{5,9},{9,13},{2,6},{6,10},{10,14},{3,7},{... | collective-permute-start | bytes 3145736 | tf_op jit(solution)/shard_map/ppermute | solution.py:43
  359.3 60.2 %collective-permute-start.34 = (bf16[4,512,256]{2,1,0:T(8,128)(2,1)S(1)}, bf16[4,512,256]{2,1,0:T(8,128)(2,1)S(1)}, u32[]{:S(2)}, u32[]{:S(2)}) collective-permute-start(bf16[4,512,256]{2,1,0:T(8,128)(2,1)S(1)} %get-tuple-element.74), channel_id=1, source_target_pairs={{0,4},{4,8},{1,5},{5,9},{2,6},{6,10},{3,7},{7,11},{16,20},{20,24},... | collective-permute-start | bytes 3145736 | tf_op jit(solution)/shard_map/ppermute | solution.py:43
  376.8 53.7 %collective-permute-start.29 = (bf16[4,512,256]{2,1,0:T(8,128)(2,1)}, bf16[4,512,256]{2,1,0:T(8,128)(2,1)}, u32[]{:S(2)}, u32[]{:S(2)}) collective-permute-start(bf16[4,512,256]{2,1,0:T(8,128)(2,1)} %collective-permute-done.28.rest_4_), channel_id=1, source_target_pairs={{4,0},{5,1},{6,2},{7,3},{20,16},{21,17},{22,18},{23,19}} | collective-permute-start | bytes 3145736 | tf_op jit(solution)/shard_map/ppermute | solution.py:30
  378.1 58.4 %collective-permute-start.31 = (bf16[4,512,256]{2,1,0:T(8,128)(2,1)}, bf16[4,512,256]{2,1,0:T(8,128)(2,1)}, u32[]{:S(2)}, u32[]{:S(2)}) collective-permute-start(bf16[4,512,256]{2,1,0:T(8,128)(2,1)} %collective-permute-done.30.rest_3_), channel_id=1, source_target_pairs={{8,12},{9,13},{10,14},{11,15},{24,28},{25,29},{26,30},{27,31}} | collective-permute-start | bytes 3145736 | tf_op jit(solution)/shard_map/ppermute | solution.py:29
  379.8 86.9 %collective-permute-start.40 = (bf16[4,512,256]{2,1,0:T(8,128)(2,1)}, bf16[4,512,256]{2,1,0:T(8,128)(2,1)}, u32[]{:S(2)}, u32[]{:S(2)}) collective-permute-start(bf16[4,512,256]{2,1,0:T(8,128)(2,1)} %collective-permute-done.39.rest_6_), channel_id=1, source_target_pairs={{4,0},{8,4},{5,1},{9,5},{6,2},{10,6},{7,3},{11,7},{20,16},{24,20},... | collective-permute-start | bytes 3145736 | tf_op jit(solution)/shard_map/ppermute | solution.py:30
  399.3 68.1 %collective-permute-start.42 = (bf16[4,512,256]{2,1,0:T(8,128)(2,1)}, bf16[4,512,256]{2,1,0:T(8,128)(2,1)}, u32[]{:S(2)}, u32[]{:S(2)}) collective-permute-start(bf16[4,512,256]{2,1,0:T(8,128)(2,1)} %collective-permute-done.38.rest_1_), channel_id=1, source_target_pairs={{4,8},{8,12},{5,9},{9,13},{6,10},{10,14},{7,11},{11,15},{20,24},{2... | collective-permute-start | bytes 3145736 | tf_op jit(solution)/shard_map/ppermute | solution.py:29
  419.5 49.2 %collective-permute-start.37 = (bf16[4,512,256]{2,1,0:T(8,128)(2,1)}, bf16[4,512,256]{2,1,0:T(8,128)(2,1)S(1)}, u32[]{:S(2)}, u32[]{:S(2)}) collective-permute-start(bf16[4,512,256]{2,1,0:T(8,128)(2,1)} %add.272), channel_id=1, source_target_pairs={{4,0},{8,4},{12,8},{5,1},{9,5},{13,9},{6,2},{10,6},{14,10},{7,3},{... | collective-permute-start | bytes 3145736 | tf_op jit(solution)/shard_map/ppermute | solution.py:44
  430.5 41.6 %collective-permute-start.35 = (bf16[4,512,256]{2,1,0:T(8,128)(2,1)}, bf16[4,512,256]{2,1,0:T(8,128)(2,1)}, u32[]{:S(2)}, u32[]{:S(2)}) collective-permute-start(bf16[4,512,256]{2,1,0:T(8,128)(2,1)} %add.267), channel_id=1, source_target_pairs={{0,4},{4,8},{8,12},{1,5},{5,9},{9,13},{2,6},{6,10},{10,14},{3,7},{... | collective-permute-start | bytes 3145736 | tf_op jit(solution)/shard_map/ppermute | solution.py:43
  528.9 177.0 %reduce-scatter.2.cloned.1.call-start = ((), (), s32[]{:S(2)}) async-start(), calls=%async_computation.2 | async-start | bytes 7864320 | tf_op jit(solution)/shard_map/reduce_scatter | solution.py:198
  535.0 52.3 %collective-permute-start.48 = (bf16[4,512,256]{2,1,0:T(8,128)(2,1)}, bf16[4,512,256]{2,1,0:T(8,128)(2,1)}, u32[]{:S(2)}, u32[]{:S(2)}) collective-permute-start(bf16[4,512,256]{2,1,0:T(8,128)(2,1)} %get-tuple-element.52), channel_id=1, source_target_pairs={{0,4},{1,5},{2,6},{3,7},{16,20},{17,21},{18,22},{19,23}} | collective-permute-start | bytes 3145736 | tf_op jit(solution)/shard_map/ppermute | solution.py:43
  540.3 48.6 %collective-permute-start.51 = (bf16[4,512,256]{2,1,0:T(8,128)(2,1)}, bf16[4,512,256]{2,1,0:T(8,128)(2,1)}, u32[]{:S(2)}, u32[]{:S(2)}) collective-permute-start(bf16[4,512,256]{2,1,0:T(8,128)(2,1)} %get-tuple-element.50), channel_id=1, source_target_pairs={{12,8},{13,9},{14,10},{15,11},{28,24},{29,25},{30,26},{31,27}} | collective-permute-start | bytes 3145736 | tf_op jit(solution)/shard_map/ppermute | solution.py:44
  569.7 32.6 %collective-permute-start.44 = (bf16[4,512,256]{2,1,0:T(8,128)(2,1)}, bf16[4,512,256]{2,1,0:T(8,128)(2,1)}, u32[]{:S(2)}, u32[]{:S(2)}) collective-permute-start(bf16[4,512,256]{2,1,0:T(8,128)(2,1)} %get-tuple-element.69), channel_id=1, source_target_pairs={{0,4},{4,8},{1,5},{5,9},{2,6},{6,10},{3,7},{7,11},{16,20},{20,24},... | collective-permute-start | bytes 3145736 | tf_op jit(solution)/shard_map/ppermute | solution.py:43
  579.8 30.8 %collective-permute-start.46 = (bf16[4,512,256]{2,1,0:T(8,128)(2,1)}, bf16[4,512,256]{2,1,0:T(8,128)(2,1)}, u32[]{:S(2)}, u32[]{:S(2)}) collective-permute-start(bf16[4,512,256]{2,1,0:T(8,128)(2,1)} %get-tuple-element.70), channel_id=1, source_target_pairs={{8,4},{12,8},{9,5},{13,9},{10,6},{14,10},{11,7},{15,11},{24,20},{2... | collective-permute-start | bytes 3145736 | tf_op jit(solution)/shard_map/ppermute | solution.py:44
  582.5 32.0 %collective-permute-start.55 = (bf16[2048,128]{0,1:T(8,128)(2,1)}, bf16[2048,128]{0,1:T(8,128)(2,1)}, u32[]{:S(2)}, u32[]{:S(2)}) collective-permute-start(bf16[2048,128]{0,1:T(8,128)(2,1)} %get-tuple-element.65), channel_id=1, source_target_pairs={{0,4},{4,8},{1,5},{5,9},{2,6},{6,10},{3,7},{7,11},{16,20},{20,24},... | collective-permute-start | bytes 1572872 | tf_op jit(solution)/shard_map/ppermute | solution.py:43
  587.4 28.9 %collective-permute-start.58 = (bf16[2048,128]{0,1:T(8,128)(2,1)}, bf16[2048,128]{0,1:T(8,128)(2,1)}, u32[]{:S(2)}, u32[]{:S(2)}) collective-permute-start(bf16[2048,128]{0,1:T(8,128)(2,1)} %get-tuple-element.66), channel_id=1, source_target_pairs={{8,4},{12,8},{9,5},{13,9},{10,6},{14,10},{11,7},{15,11},{24,20},{2... | collective-permute-start | bytes 1572872 | tf_op jit(solution)/shard_map/ppermute | solution.py:44
  592.1 44.0 %collective-permute-start.49 = (bf16[4,512,256]{2,1,0:T(8,128)(2,1)}, bf16[4,512,256]{2,1,0:T(8,128)(2,1)}, u32[]{:S(2)}, u32[]{:S(2)}) collective-permute-start(bf16[4,512,256]{2,1,0:T(8,128)(2,1)} %get-tuple-element.71), channel_id=1, source_target_pairs={{0,4},{4,8},{1,5},{5,9},{2,6},{6,10},{3,7},{7,11},{16,20},{20,24},... | collective-permute-start | bytes 3145736 | tf_op jit(solution)/shard_map/ppermute | solution.py:43
  605.1 69.1 %collective-permute-start.45 = (bf16[4,512,256]{2,1,0:T(8,128)(2,1)}, bf16[4,512,256]{2,1,0:T(8,128)(2,1)}, u32[]{:S(2)}, u32[]{:S(2)}) collective-permute-start(bf16[4,512,256]{2,1,0:T(8,128)(2,1)} %add.285), channel_id=1, source_target_pairs={{0,4},{4,8},{8,12},{1,5},{5,9},{9,13},{2,6},{6,10},{10,14},{3,7},{... | collective-permute-start | bytes 3145736 | tf_op jit(solution)/shard_map/ppermute | solution.py:43
  613.1 61.1 %collective-permute-start.47 = (bf16[4,512,256]{2,1,0:T(8,128)(2,1)}, bf16[4,512,256]{2,1,0:T(8,128)(2,1)}, u32[]{:S(2)}, u32[]{:S(2)}) collective-permute-start(bf16[4,512,256]{2,1,0:T(8,128)(2,1)} %add.288), channel_id=1, source_target_pairs={{4,0},{8,4},{12,8},{5,1},{9,5},{13,9},{6,2},{10,6},{14,10},{7,3},{... | collective-permute-start | bytes 3145736 | tf_op jit(solution)/shard_map/ppermute | solution.py:44
  614.6 29.6 %collective-permute-start.52 = (bf16[4,512,256]{2,1,0:T(8,128)(2,1)}, bf16[4,512,256]{2,1,0:T(8,128)(2,1)}, u32[]{:S(2)}, u32[]{:S(2)}) collective-permute-start(bf16[4,512,256]{2,1,0:T(8,128)(2,1)} %get-tuple-element.72), channel_id=1, source_target_pairs={{8,4},{12,8},{9,5},{13,9},{10,6},{14,10},{11,7},{15,11},{24,20},{2... | collective-permute-start | bytes 3145736 | tf_op jit(solution)/shard_map/ppermute | solution.py:44
  618.6 51.6 %collective-permute-start.56 = (bf16[2048,128]{0,1:T(8,128)(2,1)}, bf16[2048,128]{0,1:T(8,128)(2,1)S(1)}, u32[]{:S(2)}, u32[]{:S(2)}) collective-permute-start(bf16[2048,128]{0,1:T(8,128)(2,1)} %get-tuple-element.63), channel_id=1, source_target_pairs={{0,4},{4,8},{8,12},{1,5},{5,9},{9,13},{2,6},{6,10},{10,14},{3,7},{... | collective-permute-start | bytes 1572872 | tf_op jit(solution)/shard_map/ppermute | solution.py:43
  636.1 35.4 %collective-permute-start.59 = (bf16[2048,128]{0,1:T(8,128)(2,1)}, bf16[2048,128]{0,1:T(8,128)(2,1)}, u32[]{:S(2)}, u32[]{:S(2)}) collective-permute-start(bf16[2048,128]{0,1:T(8,128)(2,1)} %get-tuple-element.64), channel_id=1, source_target_pairs={{4,0},{8,4},{12,8},{5,1},{9,5},{13,9},{6,2},{10,6},{14,10},{7,3},{... | collective-permute-start | bytes 1572872 | tf_op jit(solution)/shard_map/ppermute | solution.py:44
  644.2 45.7 %collective-permute-start.50 = (bf16[4,512,256]{2,1,0:T(8,128)(2,1)}, bf16[4,512,256]{2,1,0:T(8,128)(2,1)}, u32[]{:S(2)}, u32[]{:S(2)}) collective-permute-start(bf16[4,512,256]{2,1,0:T(8,128)(2,1)} %add.291), channel_id=1, source_target_pairs={{0,4},{4,8},{8,12},{1,5},{5,9},{9,13},{2,6},{6,10},{10,14},{3,7},{... | collective-permute-start | bytes 3145736 | tf_op jit(solution)/shard_map/ppermute | solution.py:43
  (62 other events, 1183.8 us)
Sparse Core Ops, SparseCore 0:
  10.2 49.0 all-gather.1
  529.0 32.2 all-reduce.2
  564.0 58.3 reduce-scatter.1

commit v3 on v2

--- a/solution.py
+++ b/solution.py
@@ -9,7 +9,7 @@
 
 SQRT_HALF = 0.7071067811865476
 INV_ROOT_TWO_PI = 0.3989422804014327
-CHUNKS = 4
+CHUNKS = 3
 F32 = jnp.float32
 BF16 = jnp.bfloat16
 
@@ -46,16 +46,21 @@
     return terms[0].astype(F32) + got_left.astype(F32) + got_right.astype(F32), steps
 
 
-def chunk_kernel(n, slots, bs, first, base, where_ref, pattern_ref, x_ref, xt_ref, ra_ref, rat_ref, cot_ref, *rest):
+def chunk_kernel(n, slots, bs, first, last, base, where_ref, pattern_ref, x_ref, xt_ref, ra_ref, rat_ref, cot_ref, *rest):
     own_ref = rest[0]
     pairs = [(rest[1 + 2 * i], rest[2 + 2 * i]) for i in range(n - 1)]
     rest = rest[1 + 2 * (n - 1) :]
     if not first:
         acc_in, _ = rest[:2]
         rest = rest[2:]
-    hid_ref, acc_ref = rest[:2]
-    term_refs = rest[2 : 2 + n]
-    w_ref, r_ref, bt_ref = rest[2 + n :]
+    if last:
+        hid_ref, spread_ref, rank_ref = rest[:3]
+        term_refs = rest[3 : 3 + n]
+        w_ref, r_ref, bt_ref, acc_ref = rest[3 + n :]
+    else:
+        hid_ref, acc_ref = rest[:2]
+        term_refs = rest[2 : 2 + n]
+        w_ref, r_ref, bt_ref = rest[2 + n :]
     step = pl.program_id(0)
     me = where_ref[0]
     cs = bs // n
@@ -105,16 +110,22 @@
     for k in range(slots):
         acc_ref[:, pl.ds(starts[k], bs)] += lax.dot_general(grad, w_ref[k], across, preferred_element_type=F32)
     acc_ref[:, width:] += lax.dot_general(grad, r_ref[...], across, preferred_element_type=F32)
-
-
-def run_chunk(n, slots, bs, base, cj, where, pattern, x, xt, ra, rat, cot, own, pairs, carried):
+    if last:
+
+        @pl.when(step == pl.num_programs(0) - 1)
+        def _():
+            spread_ref[...] = acc_ref[:, :width].astype(BF16)
+            rank_ref[...] = acc_ref[:, width:].astype(BF16)
+
+
+def run_chunk(n, slots, bs, base, cj, last, where, pattern, x, xt, ra, rat, cot, own, pairs, carried):
     tok = x.shape[0]
     rank = ra.shape[1]
     rows = own.shape[1]
     first = carried is None
 
     def whole(a):
-        return pl.BlockSpec(a.shape, lambda i, *_: (0, 0))
+        return pl.BlockSpec(a.shape, lambda i, *_: (0, 0), pipeline_mode=pl.Buffered(1))
 
     cols = pl.BlockSpec((tok, bs), lambda i, *_: (0, base + i))
     pack = pl.BlockSpec((1, rows, bs), lambda i, *_: (i, 0, 0))
@@ -123,31 +134,39 @@
     specs = [whole(x), whole(xt), whole(ra), whole(rat), cols, pack_own] + [pack] * (2 * (n - 1))
     aliases = {}
     if not first:
-        aliases = {2 + len(ins): 1, 3 + len(ins): 0}
+        aliases = {3 + len(ins): 0} if last else {2 + len(ins): 1, 3 + len(ins): 0}
         ins += list(carried)
         specs += [pl.BlockSpec(memory_space=pl.ANY)] * 2
     acc_shape = (tok, x.shape[1] + rank)
+    if last:
+        sums = [(tok, x.shape[1]), (tok, rank)]
+        sum_type = BF16
+    else:
+        sums = [acc_shape]
+        sum_type = F32
     madds = tok * bs * bs * slots * 3 + tok * rank * bs * 3
     out = pl.pallas_call(
-        functools.partial(chunk_kernel, n, slots, bs, first, base),
+        functools.partial(chunk_kernel, n, slots, bs, first, last, base),
         grid_spec=pltpu.PrefetchScalarGridSpec(
             num_scalar_prefetch=2,
             grid=(cj,),
             in_specs=specs,
-            out_specs=[cols, pl.BlockSpec(acc_shape, lambda i, *_: (0, 0))] + [pack] * n,
+            out_specs=[cols] + [pl.BlockSpec(shape, lambda i, *_: (0, 0)) for shape in sums] + [pack] * n,
             scratch_shapes=[
                 pltpu.VMEM((slots, bs, bs), BF16),
                 pltpu.VMEM((rank, bs), BF16),
                 pltpu.VMEM((slots, bs, bs), BF16),
-            ],
+            ]
+            + ([pltpu.VMEM(acc_shape, F32)] if last else []),
         ),
-        out_shape=[jax.ShapeDtypeStruct(cot.shape, BF16), jax.ShapeDtypeStruct(acc_shape, F32)]
+        out_shape=[jax.ShapeDtypeStruct(cot.shape, BF16)]
+        + [jax.ShapeDtypeStruct(shape, sum_type) for shape in sums]
         + [jax.ShapeDtypeStruct((cj, rows, bs), BF16)] * n,
         input_output_aliases=aliases,
         compiler_params=pltpu.CompilerParams(vmem_limit_bytes=60 * 1024 * 1024),
         cost_estimate=pl.CostEstimate(flops=2 * madds * cj, bytes_accessed=50_000_000, transcendentals=0),
     )(where, pattern, *ins)
-    return out[0], out[1], out[2:]
+    return out[0], out[1 : 1 + len(sums)], out[1 + len(sums) :]
 
 
 def per_device(tokens, pattern, blocks, left_factor, right_factor, cotangent):
@@ -155,18 +174,18 @@
     local_cols, slots, cs, bs = blocks.shape
     rs = right_factor.shape[0]
     rw = left_factor.shape[1]
-    cj = local_cols // CHUNKS
+    bounds = [-(-local_cols * c // CHUNKS) for c in range(CHUNKS + 1)]
     me = lax.axis_index("dp").astype(jnp.int32).reshape(1)
     local_pattern = lax.dynamic_slice_in_dim(pattern, lax.axis_index("tensor") * local_cols, local_cols, 0)
 
-    left_pairs, _ = line_gather(left_factor, n)
+    left_pairs, waits = line_gather(left_factor, n)
     packed = jnp.concatenate(
         [blocks.reshape(local_cols, slots * cs, bs), right_factor.reshape(rs, local_cols, bs).transpose(1, 0, 2)], axis=1
     )
     gathered = []
-    waits = ()
     for c in range(CHUNKS):
-        part = lax.dynamic_slice_in_dim(packed, after(jnp.int32(c * cj), *waits), cj, 0)
+        lo, hi = bounds[c : c + 2]
+        part = lax.dynamic_slice_in_dim(packed, after(jnp.int32(lo), *waits), hi - lo, 0)
         pairs, waits = line_gather(part, n)
         gathered.append(pairs)
 
@@ -185,25 +204,25 @@
             where = after(where, *steps[c - 1][0])
         if c >= 2:
             where = after(where, *steps[c - 2][-1])
+        lo, hi = bounds[c : c + 2]
         hidden, acc, terms = run_chunk(
-            n, slots, bs, c * cj, cj, where, local_pattern, x, xt, rank_acts, rank_acts_t, cotangent, packed, gathered[c], carried
+            n, slots, bs, lo, hi - lo, c == CHUNKS - 1, where, local_pattern, x, xt, rank_acts, rank_acts_t, cotangent, packed, gathered[c], carried
         )
-        carried = (acc, hidden)
+        carried = (acc[0], hidden)
         total, got = line_scatter(list(terms), n)
         sums.append(total)
         steps.append(got)
 
-    width = x.shape[1]
-    rank_grad = lax.psum(acc[:, width:].astype(BF16), "tensor")
-    token_part = lax.psum_scatter(acc[:, :width].astype(BF16), "tensor", scatter_dimension=1, tiled=True).astype(F32)
+    rank_grad = lax.psum(acc[1], "tensor")
+    token_part = lax.psum_scatter(acc[0], "tensor", scatter_dimension=1, tiled=True).astype(F32)
     left_term = lax.dot_general(tokens, rank_grad, (((0,), (0,)), ((), ())), preferred_element_type=F32).astype(BF16)
     left_terms = [left_term[:, ((n - r) % n) * rw : ((n - r) % n + 1) * rw] for r in range(n)]
     left_grad, _ = line_scatter(left_terms, n)
     token_grad = token_part + lax.dot_general(
         rank_grad, left_rot, (((1,), (1,)), ((), ())), preferred_element_type=F32
     )
-    block_grad = jnp.concatenate([s[:, : slots * cs].reshape(cj, slots, cs, bs) for s in sums], axis=0)
-    right_grad = jnp.concatenate([s[:, slots * cs :].transpose(1, 0, 2).reshape(rs, cj * bs) for s in sums], axis=1)
+    block_grad = jnp.concatenate([s[:, : slots * cs].reshape(-1, slots, cs, bs) for s in sums], axis=0)
+    right_grad = jnp.concatenate([s[:, slots * cs :].transpose(1, 0, 2).reshape(rs, -1) for s in sums], axis=1)
     return (hidden, token_grad, block_grad, left_grad, right_grad)
 
 

time: 720 us -> 691 us (0.960)
  waiting for transfers between devices: 269 us -> 315 us
  starting transfers between devices: 163 us -> 121 us
  Pallas kernels: 104 us -> 86.8 us
  other arithmetic: 62 us -> 54.1 us
    ppermute x15 -> x12, waiting for transfers between devices: 36.7 us -> 90.6 us  [line_gather(): lax.ppermute(own if m == 1 else from_left[m - 1], 'dp', right_pairs)]
    ppermute x15 -> x12, waiting for transfers between devices: 123 us -> 83.1 us  [line_scatter(): got_left = lax.ppermute(to_right, 'dp', right_pairs)]
    ppermute x15 -> x12, starting transfers between devices: 81 us -> 60.6 us  [line_scatter(): got_left = lax.ppermute(to_right, 'dp', right_pairs)]
    pallas_call x4 -> x3, Pallas kernels: 104 us -> 86.8 us  [run_chunk(): pl.pallas_call(functools.partial(chunk_kernel, n, slots, bs, first, last,...]
    ppermute x15 -> x12, waiting for transfers between devices: 85.7 us -> 101 us  [line_gather(): lax.ppermute(own if m == 1 else from_right[m - 1], 'dp', left_pairs)]
    ppermute x15 -> x12, starting transfers between devices: 43.6 us -> 29.4 us  [line_gather(): lax.ppermute(own if m == 1 else from_left[m - 1], 'dp', right_pairs)]
    ppermute x15 -> x12, waiting for transfers between devices: 3.36 us -> 14.6 us  [line_scatter(): got_right = lax.ppermute(to_left, 'dp', left_pairs)]
    another operation x1 -> x0, other arithmetic: 8.22 us -> none
  transfers between devices with their start and end apart: 63 -> 51, of which waited for: 20 -> 18; matrix products, arithmetic and copies ran while one was open for 14% -> 14% of each run, Pallas kernels for 11% -> 8%
where the time goes in v3:
time: 691 us; the launch traced here: 685 us
  waiting for transfers between devices  315 us (46%)
  starting transfers between devices  121 us (18%)
  Pallas kernels  86.8 us (13%)
  other arithmetic  54.1 us (8%)
  local copies, waits for them, and re-layouts  48.5 us (7%)
  between operations  30.3 us (4%)
  blocking collectives  20.4 us (3%)
  matrix products  9.13 us (1%)
    ppermute x12, waiting for transfers between devices, line_gather(): lax.ppermute(own if m == 1 else from_right[m - 1], 'dp', left_pairs)  101 us
    ppermute x12, waiting for transfers between devices, line_gather(): lax.ppermute(own if m == 1 else from_left[m - 1], 'dp', right_pairs)  90.6 us
    pallas_call x3, Pallas kernels, run_chunk(): pl.pallas_call(functools.partial(chunk_kernel, n, slots, bs, first, last,...  86.8 us
    ppermute x12, waiting for transfers between devices, line_scatter(): got_left = lax.ppermute(to_right, 'dp', right_pairs)  83.1 us
    ppermute x12, starting transfers between devices, line_scatter(): got_left = lax.ppermute(to_right, 'dp', right_pairs)  60.6 us
    ppermute x12, starting transfers between devices, line_gather(): lax.ppermute(own if m == 1 else from_left[m - 1], 'dp', right_pairs)  29.4 us
    psum x1, waiting for transfers between devices, per_device(): rank_grad = lax.psum(acc[1], 'tensor')  24.3 us
    psum x1, blocking collectives, per_device(): lax.psum(jnp.dot(tokens, left_rot, preferred_element_type=F32), 'tensor')  20.4 us
  transfers between devices with their start and end apart: 51, of which 18 were waited for; matrix products, arithmetic and copies ran while one was open for 14% of the time, Pallas kernels for 8%

profile of v3, /device:TPU:0, one launch (start us, length us, event | category | flops | bytes accessed | tf_op | source)
XLA Modules:
  0.0 684.7 jit_solution(16827032612560600648)
XLA Ops:
  7.2 2.6 copy.24
  9.9 6.0 collective-permute-start
  17.2 9.4 %collective-permute-done = bf16[2048,128]{1,0:T(8,128)(2,1)} collective-permute-done((bf16[2048,128]{1,0:T(8,128)(2,1)}, bf16[2048,128]{1,0:T(8,128)(2,1)}, u32[]{:S(2)}, u32[]{:S(2)}) %collective-permute-start) | collective-permute-done | bytes 524320 | tf_op jit(solution)/shard_map/ppermute | solution.py:29
  28.0 3.5 collective-permute-done.1
  39.8 6.6 collective-permute-done.2
  49.9 3.7 collective-permute-start.6
  55.0 30.2 %collective-permute-done.6.rest_1_ = bf16[6,512,256]{2,1,0:T(8,128)(2,1)S(1)} collective-permute-done((bf16[6,512,256]{2,1,0:T(8,128)(2,1)S(1)}, bf16[6,512,256]{2,1,0:T(8,128)(2,1)S(1)}, u32[]{:S(2)}, u32[]{:S(2)}) %collective-permute-start.6) | collective-permute-done | bytes 1572896 | tf_op jit(solution)/shard_map/ppermute | solution.py:29
  93.1 32.5 %collective-permute-done.8.rest_4_ = bf16[6,512,256]{2,1,0:T(8,128)(2,1)} collective-permute-done((bf16[6,512,256]{2,1,0:T(8,128)(2,1)S(1)}, bf16[6,512,256]{2,1,0:T(8,128)(2,1)}, u32[]{:S(2)}, u32[]{:S(2)}) %collective-permute-start.8) | collective-permute-done | bytes 1572896 | tf_op jit(solution)/shard_map/ppermute | solution.py:30
  131.6 5.7 collective-permute-start.14
  141.8 28.7 %collective-permute-done.3 = bf16[2048,128]{1,0:T(8,128)(2,1)S(1)} collective-permute-done((bf16[2048,128]{1,0:T(8,128)(2,1)}, bf16[2048,128]{1,0:T(8,128)(2,1)S(1)}, u32[]{:S(2)}, u32[]{:S(2)}) %collective-permute-start.3) | collective-permute-done | bytes 524320 | tf_op jit(solution)/shard_map/ppermute | solution.py:30
  185.4 20.4 %all-reduce.4 = bf16[384,512]{0,1:T(8,128)(2,1)S(1)} all-reduce(f32[384,512]{0,1:T(8,128)} %convolution_bitcast_fusion), channel_id=1, replica_groups=mesh['pipe'=2,'dp'=4,'tensor'=4] {'tensor'}, use_global_device_ids=true, to_apply=%region_0.0 | all-reduce | flops 196608 | bytes 1179648 | tf_op jit(solution)/shard_map/psum | solution.py:195
  209.2 23.2 %collective-permute-done.16.rest_4_ = bf16[5,512,256]{2,1,0:T(8,128)(2,1)} collective-permute-done((bf16[5,512,256]{2,1,0:T(8,128)(2,1)}, bf16[5,512,256]{2,1,0:T(8,128)(2,1)}, u32[]{:S(2)}, u32[]{:S(2)}) %collective-permute-start.16) | collective-permute-done | bytes 1310752 | tf_op jit(solution)/shard_map/ppermute | solution.py:30
  238.3 8.6 %copy.27.x_ref = bf16[384,8192]{1,0:T(8,128)(2,1)} copy(bf16[384,8192]{0,1:T(8,128)(2,1)} %all-gather.2.cloned.1.call-done) | data formatting | bytes 12582912 | tf_op jit(solution)/shard_map/all_gather | solution.py:192
  246.9 28.3 %shard_map.101 = (bf16[384,4096]{1,0:T(8,128)(2,1)}, f32[384,8704]{1,0:T(8,128)}, bf16[6,512,256]{2,1,0:T(8,128)(2,1)}, bf16[6,512,256]{2,1,0:T(8,128)(2,1)}, bf...) custom-call(s32[1]{0:T(128)} %bitcast.where_ref, s32[16,6]{1,0:T(8,128)} %copy.38.pattern_ref, ...), custom_call_target="tpu_custom_call" | custom-call | flops 7247757312 | bytes 50000000 | tf_op jit(solution)/shard_map/pallas_call | solution.py:148
  275.2 4.7 collective-permute-start.12
  285.1 51.0 %collective-permute-done.26.rest_1_ = bf16[5,512,256]{2,1,0:T(8,128)(2,1)} collective-permute-done((bf16[5,512,256]{2,1,0:T(8,128)(2,1)}, bf16[5,512,256]{2,1,0:T(8,128)(2,1)}, u32[]{:S(2)}, u32[]{:S(2)}) %collective-permute-start.26) | collective-permute-done | bytes 1310752 | tf_op jit(solution)/shard_map/ppermute | solution.py:29
  339.2 3.4 fusion.8
  347.3 11.0 %collective-permute-start.22 = (bf16[6,512,256]{2,1,0:T(8,128)(2,1)}, bf16[6,512,256]{2,1,0:T(8,128)(2,1)}, u32[]{:S(2)}, u32[]{:S(2)}) collective-permute-start(bf16[6,512,256]{2,1,0:T(8,128)(2,1)} %get-tuple-element.60), channel_id=1, source_target_pairs={{0,4},{4,8},{1,5},{5,9},{2,6},{6,10},{3,7},{7,11},{16,20},{20,24},... | collective-permute-start | bytes 4718600 | tf_op jit(solution)/shard_map/ppermute | solution.py:43
  359.4 29.8 %shard_map.102 = (bf16[384,4096]{1,0:T(8,128)(2,1)}, f32[384,8704]{1,0:T(8,128)}, bf16[5,512,256]{2,1,0:T(8,128)(2,1)}, bf16[5,512,256]{2,1,0:T(8,128)(2,1)}, bf...) custom-call(s32[1]{0:T(128)S(6)} %add.186.where_ref, ...), custom_call_target="tpu_custom_call", output_to_operand_aliasing={{1}: (14, {}), {0}: (15, {})} | custom-call | flops 6039797760 | bytes 50000000 | tf_op jit(solution)/shard_map/pallas_call | solution.py:148
  389.3 3.8 collective-permute-start.20
  396.8 10.4 %collective-permute-start.23 = (bf16[6,512,256]{2,1,0:T(8,128)(2,1)S(1)}, bf16[6,512,256]{2,1,0:T(8,128)(2,1)S(1)}, u32[]{:S(2)}, u32[]{:S(2)}) collective-permute-start(bf16[6,512,256]{2,1,0:T(8,128)(2,1)S(1)} %add.197), channel_id=1, source_target_pairs={{0,4},{4,8},{8,12},{1,5},{5,9},{9,13},{2,6},{6,10},{10,14},{3,7},{... | collective-permute-start | bytes 4718600 | tf_op jit(solution)/shard_map/ppermute | solution.py:43
  409.3 13.2 %collective-permute-done.20 = bf16[5,512,256]{2,1,0:T(8,128)(2,1)S(1)} collective-permute-done((bf16[5,512,256]{2,1,0:T(8,128)(2,1)}, bf16[5,512,256]{2,1,0:T(8,128)(2,1)S(1)}, u32[]{:S(2)}, u32[]{:S(2)}) %collective-permute-start.20) | collective-permute-done | bytes 1310752 | tf_op jit(solution)/shard_map/ppermute | solution.py:43
  427.0 11.7 %collective-permute-done.25 = bf16[6,512,256]{2,1,0:T(8,128)(2,1)S(1)} collective-permute-done((bf16[6,512,256]{2,1,0:T(8,128)(2,1)S(1)}, bf16[6,512,256]{2,1,0:T(8,128)(2,1)S(1)}, u32[]{:S(2)}, u32[]{:S(2)}) %collective-permute-start.25) | collective-permute-done | bytes 1572896 | tf_op jit(solution)/shard_map/ppermute | solution.py:44
  440.5 6.7 collective-permute-done.23
  449.7 5.9 collective-permute-done.29.rest_2_
  457.1 28.7 %shard_map.103 = (bf16[384,4096]{1,0:T(8,128)(2,1)}, bf16[384,8192]{1,0:T(8,128)(2,1)}, bf16[384,512]{1,0:T(8,128)(2,1)}, bf16[5,512,256]{2,1,0:T(8,128)(2,1)}, ...) custom-call(s32[1]{0:T(128)S(6)} %add.205.where_ref, ...), custom_call_target="tpu_custom_call", output_to_operand_aliasing={{0}: (15, {})} | custom-call | flops 6039797760 | bytes 50000000 | tf_op jit(solution)/shard_map/pallas_call | solution.py:148
  486.6 2.7 collective-permute-start.36
  491.0 4.0 fusion.9
  499.1 24.3 %all-reduce.3.cloned.1.call-done = bf16[384,512]{1,0:T(8,128)(2,1)} async-done(((bf16[384,512]{1,0:T(8,128)(2,1)}), bf16[384,512]{1,0:T(8,128)(2,1)}) %all-reduce.3.cloned.1.call-update) | async-done | bytes 393232 | tf_op jit(solution)/shard_map/psum | solution.py:216
  525.9 3.7 fusion.10
  529.6 3.4 collective-permute-start.37
  533.1 3.8 collective-permute-start.42
  539.5 2.8 add.213
  542.3 3.1 collective-permute-start.33
  545.4 2.9 add.216
  548.4 26.6 %collective-permute-done.42 = bf16[2048,128]{0,1:T(8,128)(2,1)S(1)} collective-permute-done((bf16[2048,128]{0,1:T(8,128)(2,1)S(1)}, bf16[2048,128]{0,1:T(8,128)(2,1)S(1)}, u32[]{:S(2)}, u32[]{:S(2)}) %collective-permute-start.42) | collective-permute-done | bytes 524320 | tf_op jit(solution)/shard_map/ppermute | solution.py:43
  577.4 5.8 collective-permute-start.43
  587.8 2.4 copy.33
  590.2 2.7 add.219
  593.0 4.4 collective-permute-start.38
  597.4 3.1 add.222
  600.5 13.9 %collective-permute-done.43 = bf16[2048,128]{0,1:T(8,128)(2,1)} collective-permute-done((bf16[2048,128]{0,1:T(8,128)(2,1)}, bf16[2048,128]{0,1:T(8,128)(2,1)}, u32[]{:S(2)}, u32[]{:S(2)}) %collective-permute-start.43) | collective-permute-done | bytes 524320 | tf_op jit(solution)/shard_map/ppermute | solution.py:43
  618.1 5.0 collective-permute-start.44
  629.2 22.6 %collective-permute-done.44 = bf16[2048,128]{0,1:T(8,128)(2,1)S(1)} collective-permute-done((bf16[2048,128]{0,1:T(8,128)(2,1)}, bf16[2048,128]{0,1:T(8,128)(2,1)S(1)}, u32[]{:S(2)}, u32[]{:S(2)}) %collective-permute-start.44) | collective-permute-done | bytes 524320 | tf_op jit(solution)/shard_map/ppermute | solution.py:43
  652.6 2.9 collective-permute-done.47
  664.6 3.0 copy.37
  667.7 5.9 pad_maximum_fusion.1
  673.6 4.6 convert_add_fusion.1
  (204 shorter events, 111.0 us)
Async XLA Ops:
  7.2 231.1 %all-gather.2.cloned.1.call-start = ((), (), s32[]{:S(2)}) async-start(), calls=%async_computation.1 | async-start | bytes 7864320 | tf_op jit(solution)/shard_map/all_gather | solution.py:192
  9.8 513.6 %all-reduce.3.cloned.1.call-start = ((), (), s32[]{:S(2)}) async-start(), calls=%async_computation.3 | async-start | bytes 786432 | tf_op jit(solution)/shard_map/psum | solution.py:216
  9.9 16.7 %collective-permute-start = (bf16[2048,128]{1,0:T(8,128)(2,1)}, bf16[2048,128]{1,0:T(8,128)(2,1)}, u32[]{:S(2)}, u32[]{:S(2)}) collective-permute-start(bf16[2048,128]{1,0:T(8,128)(2,1)} %param.9), channel_id=1, source_target_pairs={{0,4},{4,8},{8,12},{1,5},{5,9},{9,13},{2,6},{6,10},{10,14},{3,7},{... | collective-permute-start | bytes 1572872 | tf_op jit(solution)/shard_map/ppermute | solution.py:29
  15.9 15.6 %collective-permute-start.1 = (bf16[2048,128]{1,0:T(8,128)(2,1)}, bf16[2048,128]{1,0:T(8,128)(2,1)}, u32[]{:S(2)}, u32[]{:S(2)}) collective-permute-start(bf16[2048,128]{1,0:T(8,128)(2,1)} %param.9), channel_id=1, source_target_pairs={{4,0},{8,4},{12,8},{5,1},{9,5},{13,9},{6,2},{10,6},{14,10},{7,3},{... | collective-permute-start | bytes 1572872 | tf_op jit(solution)/shard_map/ppermute | solution.py:30
  49.9 35.2 %collective-permute-start.6 = (bf16[6,512,256]{2,1,0:T(8,128)(2,1)S(1)}, bf16[6,512,256]{2,1,0:T(8,128)(2,1)S(1)}, u32[]{:S(2)}, u32[]{:S(2)}) collective-permute-start(bf16[6,512,256]{2,1,0:T(8,128)(2,1)S(1)} %fusion.1), channel_id=1, source_target_pairs={{0,4},{4,8},{8,12},{1,5},{5,9},{9,13},{2,6},{6,10},{10,14},{3,7},{... | collective-permute-start | bytes 4718600 | tf_op jit(solution)/shard_map/ppermute | solution.py:29
  53.7 35.7 %collective-permute-start.7 = (bf16[6,512,256]{2,1,0:T(8,128)(2,1)S(1)}, bf16[6,512,256]{2,1,0:T(8,128)(2,1)S(1)}, u32[]{:S(2)}, u32[]{:S(2)}) collective-permute-start(bf16[6,512,256]{2,1,0:T(8,128)(2,1)S(1)} %fusion.1), channel_id=1, source_target_pairs={{4,0},{8,4},{12,8},{5,1},{9,5},{13,9},{6,2},{10,6},{14,10},{7,3},{... | collective-permute-start | bytes 4718600 | tf_op jit(solution)/shard_map/ppermute | solution.py:30
  89.3 36.2 %collective-permute-start.8 = (bf16[6,512,256]{2,1,0:T(8,128)(2,1)S(1)}, bf16[6,512,256]{2,1,0:T(8,128)(2,1)}, u32[]{:S(2)}, u32[]{:S(2)}) collective-permute-start(bf16[6,512,256]{2,1,0:T(8,128)(2,1)S(1)} %collective-permute-done.7.rest_6_), channel_id=1, source_target_pairs={{4,0},{8,4},{5,1},{9,5},{6,2},{10,6},{7,3},{11,7},{20,16},{24,20},... | collective-permute-start | bytes 4718600 | tf_op jit(solution)/shard_map/ppermute | solution.py:30
  130.3 43.8 %collective-permute-start.15 = (bf16[5,512,256]{2,1,0:T(8,128)(2,1)}, bf16[5,512,256]{2,1,0:T(8,128)(2,1)}, u32[]{:S(2)}, u32[]{:S(2)}) collective-permute-start(bf16[5,512,256]{2,1,0:T(8,128)(2,1)} %fusion.2), channel_id=1, source_target_pairs={{4,0},{8,4},{12,8},{5,1},{9,5},{13,9},{6,2},{10,6},{14,10},{7,3},{... | collective-permute-start | bytes 3932168 | tf_op jit(solution)/shard_map/ppermute | solution.py:30
  131.6 43.8 %collective-permute-start.14 = (bf16[5,512,256]{2,1,0:T(8,128)(2,1)}, bf16[5,512,256]{2,1,0:T(8,128)(2,1)}, u32[]{:S(2)}, u32[]{:S(2)}) collective-permute-start(bf16[5,512,256]{2,1,0:T(8,128)(2,1)} %fusion.2), channel_id=1, source_target_pairs={{0,4},{4,8},{8,12},{1,5},{5,9},{9,13},{2,6},{6,10},{10,14},{3,7},{... | collective-permute-start | bytes 3932168 | tf_op jit(solution)/shard_map/ppermute | solution.py:29
  137.3 33.2 %collective-permute-start.3 = (bf16[2048,128]{1,0:T(8,128)(2,1)}, bf16[2048,128]{1,0:T(8,128)(2,1)S(1)}, u32[]{:S(2)}, u32[]{:S(2)}) collective-permute-start(bf16[2048,128]{1,0:T(8,128)(2,1)} %collective-permute-done.2), channel_id=1, source_target_pairs={{4,0},{5,1},{6,2},{7,3},{20,16},{21,17},{22,18},{23,19}} | collective-permute-start | bytes 1572872 | tf_op jit(solution)/shard_map/ppermute | solution.py:30
  138.6 42.3 %collective-permute-start.5 = (bf16[2048,128]{1,0:T(8,128)(2,1)}, bf16[2048,128]{1,0:T(8,128)(2,1)}, u32[]{:S(2)}, u32[]{:S(2)}) collective-permute-start(bf16[2048,128]{1,0:T(8,128)(2,1)} %collective-permute-done.4), channel_id=1, source_target_pairs={{8,12},{9,13},{10,14},{11,15},{24,28},{25,29},{26,30},{27,31}} | collective-permute-start | bytes 1572872 | tf_op jit(solution)/shard_map/ppermute | solution.py:29
  140.0 106.9 %collective-permute-start.11 = (bf16[6,512,256]{2,1,0:T(8,128)(2,1)}, bf16[6,512,256]{2,1,0:T(8,128)(2,1)}, u32[]{:S(2)}, u32[]{:S(2)}) collective-permute-start(bf16[6,512,256]{2,1,0:T(8,128)(2,1)} %collective-permute-done.10.rest_3_), channel_id=1, source_target_pairs={{8,12},{9,13},{10,14},{11,15},{24,28},{25,29},{26,30},{27,31}} | collective-permute-start | bytes 4718600 | tf_op jit(solution)/shard_map/ppermute | solution.py:29
  170.5 76.4 %collective-permute-start.9 = (bf16[6,512,256]{2,1,0:T(8,128)(2,1)}, bf16[6,512,256]{2,1,0:T(8,128)(2,1)}, u32[]{:S(2)}, u32[]{:S(2)}) collective-permute-start(bf16[6,512,256]{2,1,0:T(8,128)(2,1)} %collective-permute-done.8.rest_4_), channel_id=1, source_target_pairs={{4,0},{5,1},{6,2},{7,3},{20,16},{21,17},{22,18},{23,19}} | collective-permute-start | bytes 4718600 | tf_op jit(solution)/shard_map/ppermute | solution.py:30
  174.1 58.3 %collective-permute-start.16 = (bf16[5,512,256]{2,1,0:T(8,128)(2,1)}, bf16[5,512,256]{2,1,0:T(8,128)(2,1)}, u32[]{:S(2)}, u32[]{:S(2)}) collective-permute-start(bf16[5,512,256]{2,1,0:T(8,128)(2,1)} %collective-permute-done.15.rest_6_), channel_id=1, source_target_pairs={{4,0},{8,4},{5,1},{9,5},{6,2},{10,6},{7,3},{11,7},{20,16},{24,20},... | collective-permute-start | bytes 3932168 | tf_op jit(solution)/shard_map/ppermute | solution.py:30
  175.4 31.4 %collective-permute-start.18 = (bf16[5,512,256]{2,1,0:T(8,128)(2,1)}, bf16[5,512,256]{2,1,0:T(8,128)(2,1)}, u32[]{:S(2)}, u32[]{:S(2)}) collective-permute-start(bf16[5,512,256]{2,1,0:T(8,128)(2,1)} %collective-permute-done.14.rest_1_), channel_id=1, source_target_pairs={{4,8},{8,12},{5,9},{9,13},{6,10},{10,14},{7,11},{11,15},{20,24},{2... | collective-permute-start | bytes 3932168 | tf_op jit(solution)/shard_map/ppermute | solution.py:29
  237.0 47.3 %collective-permute-start.27 = (bf16[5,512,256]{2,1,0:T(8,128)(2,1)}, bf16[5,512,256]{2,1,0:T(8,128)(2,1)}, u32[]{:S(2)}, u32[]{:S(2)}) collective-permute-start(bf16[5,512,256]{2,1,0:T(8,128)(2,1)} %fusion.3), channel_id=1, source_target_pairs={{4,0},{8,4},{12,8},{5,1},{9,5},{13,9},{6,2},{10,6},{14,10},{7,3},{... | collective-permute-start | bytes 3932168 | tf_op jit(solution)/shard_map/ppermute | solution.py:30
  275.2 62.2 %collective-permute-start.12 = (bf16[6,512,256]{2,1,0:T(8,128)(2,1)}, bf16[6,512,256]{2,1,0:T(8,128)(2,1)S(1)}, u32[]{:S(2)}, u32[]{:S(2)}) collective-permute-start(bf16[6,512,256]{2,1,0:T(8,128)(2,1)} %get-tuple-element.24), channel_id=1, source_target_pairs={{0,4},{1,5},{2,6},{3,7},{16,20},{17,21},{18,22},{19,23}} | collective-permute-start | bytes 4718600 | tf_op jit(solution)/shard_map/ppermute | solution.py:43
  279.9 59.3 %collective-permute-start.13 = (bf16[6,512,256]{2,1,0:T(8,128)(2,1)}, bf16[6,512,256]{2,1,0:T(8,128)(2,1)S(1)}, u32[]{:S(2)}, u32[]{:S(2)}) collective-permute-start(bf16[6,512,256]{2,1,0:T(8,128)(2,1)} %get-tuple-element.25), channel_id=1, source_target_pairs={{12,8},{13,9},{14,10},{15,11},{28,24},{29,25},{30,26},{31,27}} | collective-permute-start | bytes 4718600 | tf_op jit(solution)/shard_map/ppermute | solution.py:44
  280.7 55.4 %collective-permute-start.26 = (bf16[5,512,256]{2,1,0:T(8,128)(2,1)}, bf16[5,512,256]{2,1,0:T(8,128)(2,1)}, u32[]{:S(2)}, u32[]{:S(2)}) collective-permute-start(bf16[5,512,256]{2,1,0:T(8,128)(2,1)} %fusion.3), channel_id=1, source_target_pairs={{0,4},{4,8},{8,12},{1,5},{5,9},{9,13},{2,6},{6,10},{10,14},{3,7},{... | collective-permute-start | bytes 3932168 | tf_op jit(solution)/shard_map/ppermute | solution.py:29
  283.0 64.2 %collective-permute-start.17 = (bf16[5,512,256]{2,1,0:T(8,128)(2,1)}, bf16[5,512,256]{2,1,0:T(8,128)(2,1)S(1)}, u32[]{:S(2)}, u32[]{:S(2)}) collective-permute-start(bf16[5,512,256]{2,1,0:T(8,128)(2,1)} %collective-permute-done.16.rest_4_), channel_id=1, source_target_pairs={{4,0},{5,1},{6,2},{7,3},{20,16},{21,17},{22,18},{23,19}} | collective-permute-start | bytes 3932168 | tf_op jit(solution)/shard_map/ppermute | solution.py:30
  284.3 74.0 %collective-permute-start.19 = (bf16[5,512,256]{2,1,0:T(8,128)(2,1)}, bf16[5,512,256]{2,1,0:T(8,128)(2,1)S(1)}, u32[]{:S(2)}, u32[]{:S(2)}) collective-permute-start(bf16[5,512,256]{2,1,0:T(8,128)(2,1)} %collective-permute-done.18.rest_3_), channel_id=1, source_target_pairs={{8,12},{9,13},{10,14},{11,15},{24,28},{25,29},{26,30},{27,31}} | collective-permute-start | bytes 3932168 | tf_op jit(solution)/shard_map/ppermute | solution.py:29
  336.1 71.1 %collective-permute-start.28 = (bf16[5,512,256]{2,1,0:T(8,128)(2,1)}, bf16[5,512,256]{2,1,0:T(8,128)(2,1)}, u32[]{:S(2)}, u32[]{:S(2)}) collective-permute-start(bf16[5,512,256]{2,1,0:T(8,128)(2,1)} %collective-permute-done.27.rest_6_), channel_id=1, source_target_pairs={{4,0},{8,4},{5,1},{9,5},{6,2},{10,6},{7,3},{11,7},{20,16},{24,20},... | collective-permute-start | bytes 3932168 | tf_op jit(solution)/shard_map/ppermute | solution.py:30
  337.4 70.6 %collective-permute-start.30 = (bf16[5,512,256]{2,1,0:T(8,128)(2,1)}, bf16[5,512,256]{2,1,0:T(8,128)(2,1)}, u32[]{:S(2)}, u32[]{:S(2)}) collective-permute-start(bf16[5,512,256]{2,1,0:T(8,128)(2,1)} %collective-permute-done.26.rest_1_), channel_id=1, source_target_pairs={{4,8},{8,12},{5,9},{9,13},{6,10},{10,14},{7,11},{11,15},{20,24},{2... | collective-permute-start | bytes 3932168 | tf_op jit(solution)/shard_map/ppermute | solution.py:29
  342.6 50.5 %collective-permute-start.24 = (bf16[6,512,256]{2,1,0:T(8,128)(2,1)}, bf16[6,512,256]{2,1,0:T(8,128)(2,1)S(1)}, u32[]{:S(2)}, u32[]{:S(2)}) collective-permute-start(bf16[6,512,256]{2,1,0:T(8,128)(2,1)} %get-tuple-element.59), channel_id=1, source_target_pairs={{8,4},{12,8},{9,5},{13,9},{10,6},{14,10},{11,7},{15,11},{24,20},{2... | collective-permute-start | bytes 4718600 | tf_op jit(solution)/shard_map/ppermute | solution.py:44
  347.3 47.7 %collective-permute-start.22 = (bf16[6,512,256]{2,1,0:T(8,128)(2,1)}, bf16[6,512,256]{2,1,0:T(8,128)(2,1)}, u32[]{:S(2)}, u32[]{:S(2)}) collective-permute-start(bf16[6,512,256]{2,1,0:T(8,128)(2,1)} %get-tuple-element.60), channel_id=1, source_target_pairs={{0,4},{4,8},{1,5},{5,9},{2,6},{6,10},{3,7},{7,11},{16,20},{20,24},... | collective-permute-start | bytes 4718600 | tf_op jit(solution)/shard_map/ppermute | solution.py:43
  389.3 33.3 %collective-permute-start.20 = (bf16[5,512,256]{2,1,0:T(8,128)(2,1)}, bf16[5,512,256]{2,1,0:T(8,128)(2,1)S(1)}, u32[]{:S(2)}, u32[]{:S(2)}) collective-permute-start(bf16[5,512,256]{2,1,0:T(8,128)(2,1)} %get-tuple-element.28), channel_id=1, source_target_pairs={{0,4},{1,5},{2,6},{3,7},{16,20},{17,21},{18,22},{19,23}} | collective-permute-start | bytes 3932168 | tf_op jit(solution)/shard_map/ppermute | solution.py:43
  393.6 45.1 %collective-permute-start.25 = (bf16[6,512,256]{2,1,0:T(8,128)(2,1)S(1)}, bf16[6,512,256]{2,1,0:T(8,128)(2,1)S(1)}, u32[]{:S(2)}, u32[]{:S(2)}) collective-permute-start(bf16[6,512,256]{2,1,0:T(8,128)(2,1)S(1)} %add.202), channel_id=1, source_target_pairs={{4,0},{8,4},{12,8},{5,1},{9,5},{13,9},{6,2},{10,6},{14,10},{7,3},{... | collective-permute-start | bytes 4718600 | tf_op jit(solution)/shard_map/ppermute | solution.py:44
  396.8 50.3 %collective-permute-start.23 = (bf16[6,512,256]{2,1,0:T(8,128)(2,1)S(1)}, bf16[6,512,256]{2,1,0:T(8,128)(2,1)S(1)}, u32[]{:S(2)}, u32[]{:S(2)}) collective-permute-start(bf16[6,512,256]{2,1,0:T(8,128)(2,1)S(1)} %add.197), channel_id=1, source_target_pairs={{0,4},{4,8},{8,12},{1,5},{5,9},{9,13},{2,6},{6,10},{10,14},{3,7},{... | collective-permute-start | bytes 4718600 | tf_op jit(solution)/shard_map/ppermute | solution.py:43
  407.2 17.9 %collective-permute-start.21 = (bf16[5,512,256]{2,1,0:T(8,128)(2,1)S(1)}, bf16[5,512,256]{2,1,0:T(8,128)(2,1)S(1)}, u32[]{:S(2)}, u32[]{:S(2)}) collective-permute-start(bf16[5,512,256]{2,1,0:T(8,128)(2,1)S(1)} %copy-done.28), channel_id=1, source_target_pairs={{12,8},{13,9},{14,10},{15,11},{28,24},{29,25},{30,26},{31,27}} | collective-permute-start | bytes 3932168 | tf_op jit(solution)/shard_map/ppermute | solution.py:44
  408.0 47.6 %collective-permute-start.29 = (bf16[5,512,256]{2,1,0:T(8,128)(2,1)}, bf16[5,512,256]{2,1,0:T(8,128)(2,1)S(1)}, u32[]{:S(2)}, u32[]{:S(2)}) collective-permute-start(bf16[5,512,256]{2,1,0:T(8,128)(2,1)} %collective-permute-done.28.rest_4_), channel_id=1, source_target_pairs={{4,0},{5,1},{6,2},{7,3},{20,16},{21,17},{22,18},{23,19}} | collective-permute-start | bytes 3932168 | tf_op jit(solution)/shard_map/ppermute | solution.py:30
  422.5 33.1 %collective-permute-start.31 = (bf16[5,512,256]{2,1,0:T(8,128)(2,1)}, bf16[5,512,256]{2,1,0:T(8,128)(2,1)S(1)}, u32[]{:S(2)}, u32[]{:S(2)}) collective-permute-start(bf16[5,512,256]{2,1,0:T(8,128)(2,1)} %collective-permute-done.30.rest_3_), channel_id=1, source_target_pairs={{8,12},{9,13},{10,14},{11,15},{24,28},{25,29},{26,30},{27,31}} | collective-permute-start | bytes 3932168 | tf_op jit(solution)/shard_map/ppermute | solution.py:29
  485.9 187.7 %reduce-scatter.2.cloned.1.call-start = ((), (), s32[]{:S(2)}) async-start(), calls=%async_computation.2 | async-start | bytes 7864320 | tf_op jit(solution)/shard_map/reduce_scatter | solution.py:217
  486.6 39.2 %collective-permute-start.36 = (bf16[5,512,256]{2,1,0:T(8,128)(2,1)}, bf16[5,512,256]{2,1,0:T(8,128)(2,1)}, u32[]{:S(2)}, u32[]{:S(2)}) collective-permute-start(bf16[5,512,256]{2,1,0:T(8,128)(2,1)} %get-tuple-element.42), channel_id=1, source_target_pairs={{0,4},{1,5},{2,6},{3,7},{16,20},{17,21},{18,22},{19,23}} | collective-permute-start | bytes 3932168 | tf_op jit(solution)/shard_map/ppermute | solution.py:43
  489.3 36.6 %collective-permute-start.39 = (bf16[5,512,256]{2,1,0:T(8,128)(2,1)}, bf16[5,512,256]{2,1,0:T(8,128)(2,1)}, u32[]{:S(2)}, u32[]{:S(2)}) collective-permute-start(bf16[5,512,256]{2,1,0:T(8,128)(2,1)} %get-tuple-element.40), channel_id=1, source_target_pairs={{12,8},{13,9},{14,10},{15,11},{28,24},{29,25},{30,26},{31,27}} | collective-permute-start | bytes 3932168 | tf_op jit(solution)/shard_map/ppermute | solution.py:44
  495.0 42.6 %collective-permute-start.32 = (bf16[5,512,256]{2,1,0:T(8,128)(2,1)}, bf16[5,512,256]{2,1,0:T(8,128)(2,1)}, u32[]{:S(2)}, u32[]{:S(2)}) collective-permute-start(bf16[5,512,256]{2,1,0:T(8,128)(2,1)} %get-tuple-element.61), channel_id=1, source_target_pairs={{0,4},{4,8},{1,5},{5,9},{2,6},{6,10},{3,7},{7,11},{16,20},{20,24},... | collective-permute-start | bytes 3932168 | tf_op jit(solution)/shard_map/ppermute | solution.py:43
  497.4 44.9 %collective-permute-start.34 = (bf16[5,512,256]{2,1,0:T(8,128)(2,1)}, bf16[5,512,256]{2,1,0:T(8,128)(2,1)}, u32[]{:S(2)}, u32[]{:S(2)}) collective-permute-start(bf16[5,512,256]{2,1,0:T(8,128)(2,1)} %get-tuple-element.62), channel_id=1, source_target_pairs={{8,4},{12,8},{9,5},{13,9},{10,6},{14,10},{11,7},{15,11},{24,20},{2... | collective-permute-start | bytes 3932168 | tf_op jit(solution)/shard_map/ppermute | solution.py:44
  529.6 53.6 %collective-permute-start.37 = (bf16[5,512,256]{2,1,0:T(8,128)(2,1)S(1)}, bf16[5,512,256]{2,1,0:T(8,128)(2,1)S(1)}, u32[]{:S(2)}, u32[]{:S(2)}) collective-permute-start(bf16[5,512,256]{2,1,0:T(8,128)(2,1)S(1)} %get-tuple-element.63), channel_id=1, source_target_pairs={{0,4},{4,8},{1,5},{5,9},{2,6},{6,10},{3,7},{7,11},{16,20},{20,24},... | collective-permute-start | bytes 3932168 | tf_op jit(solution)/shard_map/ppermute | solution.py:43
  533.1 41.9 %collective-permute-start.42 = (bf16[2048,128]{0,1:T(8,128)(2,1)S(1)}, bf16[2048,128]{0,1:T(8,128)(2,1)S(1)}, u32[]{:S(2)}, u32[]{:S(2)}) collective-permute-start(bf16[2048,128]{0,1:T(8,128)(2,1)S(1)} %get-tuple-element.57), channel_id=1, source_target_pairs={{0,4},{1,5},{2,6},{3,7},{16,20},{17,21},{18,22},{19,23}} | collective-permute-start | bytes 1572872 | tf_op jit(solution)/shard_map/ppermute | solution.py:43
  536.9 39.4 %collective-permute-start.45 = (bf16[2048,128]{0,1:T(8,128)(2,1)S(1)}, bf16[2048,128]{0,1:T(8,128)(2,1)S(1)}, u32[]{:S(2)}, u32[]{:S(2)}) collective-permute-start(bf16[2048,128]{0,1:T(8,128)(2,1)S(1)} %get-tuple-element.58), channel_id=1, source_target_pairs={{12,8},{13,9},{14,10},{15,11},{28,24},{29,25},{30,26},{31,27}} | collective-permute-start | bytes 1572872 | tf_op jit(solution)/shard_map/ppermute | solution.py:44
  537.6 55.4 %collective-permute-start.40 = (bf16[5,512,256]{2,1,0:T(8,128)(2,1)}, bf16[5,512,256]{2,1,0:T(8,128)(2,1)}, u32[]{:S(2)}, u32[]{:S(2)}) collective-permute-start(bf16[5,512,256]{2,1,0:T(8,128)(2,1)} %get-tuple-element.64), channel_id=1, source_target_pairs={{8,4},{12,8},{9,5},{13,9},{10,6},{14,10},{11,7},{15,11},{24,20},{2... | collective-permute-start | bytes 3932168 | tf_op jit(solution)/shard_map/ppermute | solution.py:44
  542.3 80.8 %collective-permute-start.33 = (bf16[5,512,256]{2,1,0:T(8,128)(2,1)}, bf16[5,512,256]{2,1,0:T(8,128)(2,1)}, u32[]{:S(2)}, u32[]{:S(2)}) collective-permute-start(bf16[5,512,256]{2,1,0:T(8,128)(2,1)} %add.213), channel_id=1, source_target_pairs={{0,4},{4,8},{8,12},{1,5},{5,9},{9,13},{2,6},{6,10},{10,14},{3,7},{... | collective-permute-start | bytes 3932168 | tf_op jit(solution)/shard_map/ppermute | solution.py:43
  575.0 49.5 %collective-permute-start.35 = (bf16[5,512,256]{2,1,0:T(8,128)(2,1)}, bf16[5,512,256]{2,1,0:T(8,128)(2,1)}, u32[]{:S(2)}, u32[]{:S(2)}) collective-permute-start(bf16[5,512,256]{2,1,0:T(8,128)(2,1)} %add.216), channel_id=1, source_target_pairs={{4,0},{8,4},{12,8},{5,1},{9,5},{13,9},{6,2},{10,6},{14,10},{7,3},{... | collective-permute-start | bytes 3932168 | tf_op jit(solution)/shard_map/ppermute | solution.py:44
  577.4 37.0 %collective-permute-start.43 = (bf16[2048,128]{0,1:T(8,128)(2,1)}, bf16[2048,128]{0,1:T(8,128)(2,1)}, u32[]{:S(2)}, u32[]{:S(2)}) collective-permute-start(bf16[2048,128]{0,1:T(8,128)(2,1)} %get-tuple-element.55), channel_id=1, source_target_pairs={{0,4},{4,8},{1,5},{5,9},{2,6},{6,10},{3,7},{7,11},{16,20},{20,24},... | collective-permute-start | bytes 1572872 | tf_op jit(solution)/shard_map/ppermute | solution.py:43
  583.2 32.5 %collective-permute-start.46 = (bf16[2048,128]{0,1:T(8,128)(2,1)}, bf16[2048,128]{0,1:T(8,128)(2,1)}, u32[]{:S(2)}, u32[]{:S(2)}) collective-permute-start(bf16[2048,128]{0,1:T(8,128)(2,1)} %get-tuple-element.56), channel_id=1, source_target_pairs={{8,4},{12,8},{9,5},{13,9},{10,6},{14,10},{11,7},{15,11},{24,20},{2... | collective-permute-start | bytes 1572872 | tf_op jit(solution)/shard_map/ppermute | solution.py:44
  593.0 65.3 %collective-permute-start.38 = (bf16[5,512,256]{2,1,0:T(8,128)(2,1)}, bf16[5,512,256]{2,1,0:T(8,128)(2,1)}, u32[]{:S(2)}, u32[]{:S(2)}) collective-permute-start(bf16[5,512,256]{2,1,0:T(8,128)(2,1)} %add.219), channel_id=1, source_target_pairs={{0,4},{4,8},{8,12},{1,5},{5,9},{9,13},{2,6},{6,10},{10,14},{3,7},{... | collective-permute-start | bytes 3932168 | tf_op jit(solution)/shard_map/ppermute | solution.py:43
  614.4 43.9 %collective-permute-start.41 = (bf16[5,512,256]{2,1,0:T(8,128)(2,1)}, bf16[5,512,256]{2,1,0:T(8,128)(2,1)}, u32[]{:S(2)}, u32[]{:S(2)}) collective-permute-start(bf16[5,512,256]{2,1,0:T(8,128)(2,1)} %add.222), channel_id=1, source_target_pairs={{4,0},{8,4},{12,8},{5,1},{9,5},{13,9},{6,2},{10,6},{14,10},{7,3},{... | collective-permute-start | bytes 3932168 | tf_op jit(solution)/shard_map/ppermute | solution.py:44
  618.1 33.7 %collective-permute-start.44 = (bf16[2048,128]{0,1:T(8,128)(2,1)}, bf16[2048,128]{0,1:T(8,128)(2,1)S(1)}, u32[]{:S(2)}, u32[]{:S(2)}) collective-permute-start(bf16[2048,128]{0,1:T(8,128)(2,1)} %get-tuple-element.53), channel_id=1, source_target_pairs={{0,4},{4,8},{8,12},{1,5},{5,9},{9,13},{2,6},{6,10},{10,14},{3,7},{... | collective-permute-start | bytes 1572872 | tf_op jit(solution)/shard_map/ppermute | solution.py:43
  623.1 32.4 %collective-permute-start.47 = (bf16[2048,128]{0,1:T(8,128)(2,1)}, bf16[2048,128]{0,1:T(8,128)(2,1)}, u32[]{:S(2)}, u32[]{:S(2)}) collective-permute-start(bf16[2048,128]{0,1:T(8,128)(2,1)} %get-tuple-element.54), channel_id=1, source_target_pairs={{4,0},{8,4},{12,8},{5,1},{9,5},{13,9},{6,2},{10,6},{14,10},{7,3},{... | collective-permute-start | bytes 1572872 | tf_op jit(solution)/shard_map/ppermute | solution.py:44
  (46 other events, 758.8 us)
Sparse Core Ops, SparseCore 0:
  10.2 49.0 all-gather.1
  486.0 37.3 all-reduce.2
  526.1 58.3 reduce-scatter.1
